TPU v7x, 32 devices: a whole 2x2x4 slice. The times are simulated.
32 devices in a mesh: section: 2 (over x), dp: 4 (over z), tensor: 4 (over y, core).
Axes of the slice: x: 2, y: 2, z: 4, core: 2. Of those that a mesh axis runs over, the one named last changes fastest.
Arguments:
- block_in: bfloat16 [2, 24, 256, 768], P('section', 'dp', 'tensor'), may hold values from -6 to 6
- lengths: int32 [24], P('dp'), may hold values from 129 to 256, as said below
- patch_mask: int32 [24, 256], P('dp'), may hold values 0 or 1
- pred_grad: bfloat16 [24, 256, 768], P('dp', 'tensor'), may hold values from -6 to 6
- w_qkv: bfloat16 [2, 3, 768, 768], P('section', None, None, 'tensor'), may hold values from -0.21875 to 0.21875
- w_out: bfloat16 [2, 768, 768], P('section', 'tensor'), may hold values from -0.875 to 0.875
- w_up: bfloat16 [2, 768, 3072], P('section', None, 'tensor'), may hold values from -0.21875 to 0.21875
- w_down: bfloat16 [2, 3072, 768], P('section', 'tensor'), may hold values from -0.109375 to 0.109375
- qv_bias: float32 [2, 2, 768], P('section', None, 'tensor'), may hold values from -1.8 to 1.8
- mlp_bias: float32 [2, 3072], P('section', 'tensor'), may hold values from -1.8 to 1.8
- norms: float32 [2, 8, 768], P('section'), may hold values from -0.9 to 1.6, as said below
Outputs:
- results: bfloat16 [2, 24, 256, 768], P('section', 'dp', 'tensor')
- grad_in: float32 [2, 24, 256, 768], P('section', 'dp', 'tensor')
- grad_qkv: float32 [2, 3, 768, 768], P('section', None, None, 'tensor')
- grad_out: float32 [2, 768, 768], P('section', 'tensor')
- grad_up: float32 [2, 768, 3072], P('section', None, 'tensor')
- grad_down: float32 [2, 3072, 768], P('section', 'tensor')
- grad_qv_bias: float32 [2, 2, 768], P('section', None, 'tensor')
- grad_mlp_bias: float32 [2, 3072], P('section', 'tensor')
- grad_norms: float32 [2, 8, 768], P('section')
Inputs may be any that keep to these rules, and one draw needn't show every extreme that they name: `lengths`: slots at or past an image's length are padding; some image has all 256 slots real. `norms`: rows 0 and 4 are norm gains, 1 and 5 norm shifts, 2 and 6 output biases, 3 and 7 layer scales.
All inputs are finite; a program needn't handle non-finite values. No bound on the sum of `patch_mask` on one device may be relied on, other than what follows from the above.
Results may differ from a plain program's by a relative error of at most 0.018.
Values may be sent and summed in bfloat16 or wider, within the bound.
A program may use at most 192 MiB of HBM per device.

v0:
```python
import jax
import jax.numpy as jnp
from jax import lax
from jax.sharding import PartitionSpec as P

D = 768
HD = 64
MB = 2


norm_epsilon = 1e-06
masked_score = -1000000000.0


def from_behind(array, axis, by):
    peers = lax.axis_size(axis)
    pairs = [(i, i + by) for i in range(peers) if 0 <= i + by < peers]
    return lax.ppermute(array, axis, pairs)


def layer_norm(tensor_in, norm_gain, norm_shift):
    row_mean = jnp.mean(tensor_in, axis=-1, keepdims=True)
    centred = tensor_in - row_mean
    spread = jnp.mean(centred * centred, axis=-1, keepdims=True)
    return centred * lax.rsqrt(spread + norm_epsilon) * norm_gain + norm_shift


def gelu_exact(tensor_in):
    return jax.nn.gelu(tensor_in, approximate=False)


def rows_product(left_side, right_side):
    return jnp.einsum("bpd,df->bpf", left_side, right_side, preferred_element_type=jnp.float32)


def rows_transposed(left_side, right_side):
    return jnp.einsum("bpf,df->bpd", left_side, right_side, preferred_element_type=jnp.float32)


def outer_sum(left_side, right_side):
    return jnp.einsum("bpd,bpf->df", left_side, right_side, preferred_element_type=jnp.float32)


def forward_block(inputs, extra_low, weights, key_ok):
    w_qkv, w_out, w_up, w_down, qv_bias, mlp_bias, norms = weights
    normed = layer_norm(inputs, norms[0], norms[1]).astype(jnp.bfloat16)
    normed_extra = layer_norm(extra_low.astype(jnp.float32), norms[0], norms[1]).astype(
        jnp.bfloat16
    )
    full_self, full_extra = (
        lax.all_gather(normed, "tensor", axis=1, tiled=True),
        lax.all_gather(normed_extra, "tensor", axis=1, tiled=True),
    )
    image_count, slot_count = (full_self.shape[0], full_self.shape[1])
    head_count = w_qkv.shape[2] // HD
    key_input = jnp.concatenate([full_extra, full_self], axis=1)
    queries = (
        (rows_product(full_self, w_qkv[0]) + qv_bias[0])
        .astype(jnp.bfloat16)
        .reshape(image_count, slot_count, head_count, HD)
    )
    keys_low = (
        rows_product(key_input, w_qkv[1])
        .astype(jnp.bfloat16)
        .reshape(image_count, 2 * slot_count, head_count, HD)
    )
    values = (
        (rows_product(key_input, w_qkv[2]) + qv_bias[1])
        .astype(jnp.bfloat16)
        .reshape(image_count, 2 * slot_count, head_count, HD)
    )
    score_scale = HD ** (-0.5)
    raw_scores = jnp.einsum(
        "bqhd,bkhd->bhqk", queries, keys_low, preferred_element_type=jnp.float32
    )
    scores = jnp.where(key_ok[:, None], raw_scores * score_scale, masked_score)
    row_top = jnp.max(scores, axis=-1, keepdims=True)
    exponent = jnp.exp(scores - row_top)
    row_total = jnp.sum(exponent, axis=-1, keepdims=True)
    attention = (exponent / row_total).astype(jnp.bfloat16)
    mixed_low = (
        jnp.einsum("bhqk,bkhd->bqhd", attention, values, preferred_element_type=jnp.float32)
        .astype(jnp.bfloat16)
        .reshape(image_count, slot_count, head_count * HD)
    )
    attended = (
        lax.psum_scatter(
            rows_product(mixed_low, w_out).astype(jnp.bfloat16),
            "tensor",
            scatter_dimension=1,
            tiled=True,
        ).astype(jnp.float32)
        + norms[2]
    )
    middle = inputs + norms[3] * attended
    normed_mid = layer_norm(middle, norms[4], norms[5]).astype(jnp.bfloat16)
    full_mid = lax.all_gather(normed_mid, "tensor", axis=1, tiled=True)
    pre_act = rows_product(full_mid, w_up) + mlp_bias
    hidden = gelu_exact(pre_act).astype(jnp.bfloat16)
    branch = (
        lax.psum_scatter(
            rows_product(hidden, w_down).astype(jnp.bfloat16),
            "tensor",
            scatter_dimension=1,
            tiled=True,
        ).astype(jnp.float32)
        + norms[6]
    )
    stored = (
        inputs,
        extra_low,
        full_self,
        key_input,
        queries,
        keys_low,
        values,
        row_top,
        row_total,
        mixed_low,
        attended,
        middle,
        full_mid,
        pre_act,
        hidden,
        branch,
    )
    return (middle + norms[7] * branch, stored)


def mlp_back(grad_out, stored, weights):
    w_qkv, w_out, w_up, w_down, qv_bias, mlp_bias, norms = weights
    (
        inputs,
        extra_low,
        full_self,
        key_input,
        queries,
        keys_low,
        values,
        row_top,
        row_total,
        mixed_low,
        attended,
        middle,
        full_mid,
        pre_act,
        hidden,
        branch,
    ) = stored
    d_final_scale = jnp.sum(grad_out * branch, axis=(0, 1))
    d_branch = norms[7] * grad_out
    d_branch_bias = jnp.sum(d_branch, axis=(0, 1))
    full_grad = lax.all_gather(d_branch.astype(jnp.bfloat16), "tensor", axis=1, tiled=True)
    d_w_down = outer_sum(hidden, full_grad)
    primal_out, gelu_back = jax.vjp(gelu_exact, pre_act)
    d_pre = gelu_back(rows_transposed(full_grad, w_down))[0]
    d_mlp_bias = jnp.sum(d_pre, axis=(0, 1))
    pre_low = d_pre.astype(jnp.bfloat16)
    d_w_up = outer_sum(full_mid, pre_low)
    d_normed_mid = lax.psum_scatter(
        rows_transposed(pre_low, w_up).astype(jnp.bfloat16),
        "tensor",
        scatter_dimension=1,
        tiled=True,
    ).astype(jnp.float32)
    primal_norm, norm_back = jax.vjp(layer_norm, middle, norms[4], norms[5])
    d_middle, gain_mid, shift_mid = norm_back(d_normed_mid)
    return (
        d_middle + grad_out,
        (d_w_up, d_w_down, d_mlp_bias),
        (gain_mid, shift_mid, d_branch_bias, d_final_scale),
    )


def attn_back(d_middle, stored, weights, key_ok):
    w_qkv, w_out, w_up, w_down, qv_bias, mlp_bias, norms = weights
    (
        inputs,
        extra_low,
        full_self,
        key_input,
        queries,
        keys_low,
        values,
        row_top,
        row_total,
        mixed_low,
        attended,
        middle,
        full_mid,
        pre_act,
        hidden,
        branch,
    ) = stored
    image_count, slot_count, head_count = (queries.shape[0], queries.shape[1], queries.shape[2])
    d_layer_scale = jnp.sum(d_middle * attended, axis=(0, 1))
    d_attended = norms[3] * d_middle
    d_out_bias = jnp.sum(d_attended, axis=(0, 1))
    full_grad = lax.all_gather(d_attended.astype(jnp.bfloat16), "tensor", axis=1, tiled=True)
    d_w_out = outer_sum(mixed_low, full_grad)
    d_mixed = (
        rows_transposed(full_grad, w_out)
        .astype(jnp.bfloat16)
        .reshape(image_count, slot_count, head_count, HD)
    )
    score_scale = HD ** (-0.5)
    raw_scores = jnp.einsum(
        "bqhd,bkhd->bhqk", queries, keys_low, preferred_element_type=jnp.float32
    )
    scores = jnp.where(key_ok[:, None], raw_scores * score_scale, masked_score)
    attention = jnp.exp(scores - row_top) / row_total
    d_attention = jnp.einsum("bqhd,bkhd->bhqk", d_mixed, values, preferred_element_type=jnp.float32)
    d_values = jnp.einsum(
        "bhqk,bqhd->bkhd",
        attention.astype(jnp.bfloat16),
        d_mixed,
        preferred_element_type=jnp.float32,
    ).reshape(image_count, 2 * slot_count, head_count * HD)
    d_scores = attention * (d_attention - jnp.sum(d_attention * attention, axis=-1, keepdims=True))
    d_raw = jnp.where(key_ok[:, None], d_scores * score_scale, 0.0).astype(jnp.bfloat16)
    d_queries = jnp.einsum(
        "bhqk,bkhd->bqhd", d_raw, keys_low, preferred_element_type=jnp.float32
    ).reshape(image_count, slot_count, head_count * HD)
    d_keys = jnp.einsum(
        "bhqk,bqhd->bkhd", d_raw, queries, preferred_element_type=jnp.float32
    ).reshape(image_count, 2 * slot_count, head_count * HD)
    d_bias = jnp.stack([jnp.sum(d_queries, axis=(0, 1)), jnp.sum(d_values, axis=(0, 1))])
    query_low = d_queries.astype(jnp.bfloat16)
    key_grad_low = d_keys.astype(jnp.bfloat16)
    value_low = d_values.astype(jnp.bfloat16)
    d_w_qkv = jnp.stack(
        [
            outer_sum(full_self, query_low),
            outer_sum(key_input, key_grad_low),
            outer_sum(key_input, value_low),
        ]
    )
    d_keyed = rows_transposed(key_grad_low, w_qkv[1]) + rows_transposed(value_low, w_qkv[2])
    d_self_part = rows_transposed(query_low, w_qkv[0]) + d_keyed[:, slot_count:]
    d_self, d_extra = (
        lax.psum_scatter(
            d_self_part.astype(jnp.bfloat16), "tensor", scatter_dimension=1, tiled=True
        ).astype(jnp.float32),
        lax.psum_scatter(
            d_keyed[:, :slot_count].astype(jnp.bfloat16), "tensor", scatter_dimension=1, tiled=True
        ).astype(jnp.float32),
    )
    primal_self, self_back = jax.vjp(layer_norm, inputs, norms[0], norms[1])
    d_in_norm, gain_self, shift_self = self_back(d_self)
    primal_extra, extra_back = jax.vjp(
        layer_norm, extra_low.astype(jnp.float32), norms[0], norms[1]
    )
    d_extra_in, gain_extra, shift_extra = extra_back(d_extra)
    return (
        d_middle + d_in_norm,
        d_extra_in,
        (d_w_qkv, d_w_out, d_bias),
        (gain_self + gain_extra, shift_self + shift_extra, d_out_bias, d_layer_scale),
    )


def select_micro(table, micro_index):
    return lax.dynamic_index_in_dim(table, micro_index, 0, keepdims=False)


def local(
    block_in, lengths, patch_mask, pred_grad, w_qkv, w_out, w_up, w_down, qv_bias, mlp_bias, norms
):
    weights = (w_qkv[0], w_out[0], w_up[0], w_down[0], qv_bias[0], mlp_bias[0], norms[0])
    section_index = lax.axis_index("section")
    regress = section_index == 1
    tensor_index = lax.axis_index("tensor")
    image_total = patch_mask.shape[0]
    slot_count = patch_mask.shape[1]
    local_rows = block_in.shape[2]
    image_count = image_total // MB
    positions = jnp.arange(slot_count, dtype=jnp.int32)
    is_valid = positions[None, :] < lengths[:, None]
    is_seen = is_valid & (patch_mask > 0)
    covered = is_valid & (patch_mask == 0)
    same_group = is_valid[:, None, :] & (is_seen[:, :, None] == is_seen[:, None, :])
    extra_ok = jnp.broadcast_to(is_seen[:, None, :] & regress, same_group.shape)
    self_ok = jnp.where(
        regress, jnp.broadcast_to(covered[:, None, :], same_group.shape), same_group
    )
    key_table = jnp.concatenate([extra_ok, self_ok], axis=-1).reshape(
        MB, image_count, slot_count, 2 * slot_count
    )
    row_start = tensor_index * local_rows
    seen_local = (
        lax.dynamic_slice_in_dim(is_seen, row_start, local_rows, 1)
        .astype(jnp.float32)
        .reshape(MB, image_count, local_rows, 1)
    )
    cover_local = (
        lax.dynamic_slice_in_dim(covered, row_start, local_rows, 1)
        .astype(jnp.float32)
        .reshape(MB, image_count, local_rows, 1)
    )
    inputs_all = block_in[0].astype(jnp.float32).reshape(MB, image_count, local_rows, D)
    upstream = pred_grad.astype(jnp.float32).reshape(MB, image_count, local_rows, D)
    arriving = jnp.zeros((image_count, local_rows, D), jnp.bfloat16)
    results = jnp.zeros((MB, image_count, local_rows, D), jnp.float32)
    kept_ticks = []
    for step_tick in range(MB + 1):
        offset = step_tick - section_index
        active = (offset >= 0) & (offset < MB)
        micro_index = jnp.clip(offset, 0, MB - 1)
        inputs = select_micro(inputs_all, micro_index)
        key_ok = select_micro(key_table, micro_index)
        layer_out, stored = forward_block(inputs, arriving, weights, key_ok)
        kept_ticks.append((inputs, arriving, key_ok, stored))
        written = lax.dynamic_update_index_in_dim(
            results, layer_out * select_micro(cover_local, micro_index), micro_index, 0
        )
        results = jnp.where(active, written, results)
        if step_tick < MB:
            arriving = from_behind(
                (layer_out * select_micro(seen_local, micro_index)).astype(jnp.bfloat16),
                "section",
                1,
            )
    returning = jnp.zeros((image_count, local_rows, D), jnp.bfloat16)
    grad_inputs = jnp.zeros_like(results)
    attn_acc = (
        jnp.zeros(w_qkv.shape[1:], jnp.float32),
        jnp.zeros(w_out.shape[1:], jnp.float32),
        jnp.zeros(qv_bias.shape[1:], jnp.float32),
    )
    mlp_acc = (
        jnp.zeros(w_up.shape[1:], jnp.float32),
        jnp.zeros(w_down.shape[1:], jnp.float32),
        jnp.zeros(mlp_bias.shape[1:], jnp.float32),
    )
    norm_acc = jnp.zeros(norms.shape[1:], jnp.float32)
    for back_tick in range(MB + 1):
        inputs, arriving, key_ok, stored = kept_ticks[MB - back_tick]
        stored = forward_block(inputs, arriving, weights, key_ok)[1]
        offset = MB - back_tick - section_index
        active = (offset >= 0) & (offset < MB)
        micro_index = jnp.clip(offset, 0, MB - 1)
        from_loss = select_micro(upstream, micro_index) * select_micro(cover_local, micro_index)
        from_next = returning.astype(jnp.float32) * select_micro(seen_local, micro_index)
        grad_out = jnp.where(regress, from_loss, from_next) * active.astype(jnp.float32)
        d_middle, mlp_terms, mlp_norms = mlp_back(grad_out, stored, weights)
        mlp_acc = jax.tree.map(jnp.add, mlp_acc, mlp_terms)
        d_inputs, d_extra, attn_terms, attn_norms = attn_back(d_middle, stored, weights, key_ok)
        attn_acc = jax.tree.map(jnp.add, attn_acc, attn_terms)
        norm_acc = norm_acc + jnp.stack(
            [
                attn_norms[0],
                attn_norms[1],
                attn_norms[2],
                attn_norms[3],
                mlp_norms[0],
                mlp_norms[1],
                mlp_norms[2],
                mlp_norms[3],
            ]
        )
        written = lax.dynamic_update_index_in_dim(grad_inputs, d_inputs, micro_index, 0)
        grad_inputs = jnp.where(active, written, grad_inputs)
        if back_tick < MB:
            returning = from_behind(d_extra.astype(jnp.bfloat16), "section", -1)
    summed = (
        lax.psum(attn_acc[0].astype(jnp.bfloat16), "dp").astype(jnp.float32),
        lax.psum(attn_acc[1].astype(jnp.bfloat16), "dp").astype(jnp.float32),
        lax.psum(attn_acc[2].astype(jnp.bfloat16), "dp").astype(jnp.float32),
        lax.psum(mlp_acc[0].astype(jnp.bfloat16), "dp").astype(jnp.float32),
        lax.psum(mlp_acc[1].astype(jnp.bfloat16), "dp").astype(jnp.float32),
        lax.psum(mlp_acc[2].astype(jnp.bfloat16), "dp").astype(jnp.float32),
    )
    attn_acc = (summed[0], summed[1], summed[2])
    mlp_acc = (summed[3], summed[4], summed[5])
    norm_sum = lax.psum(norm_acc, ("dp", "tensor"))
    results_out = results.reshape(image_total, local_rows, D).astype(jnp.bfloat16)[None]
    grad_out_in = grad_inputs.reshape(image_total, local_rows, D)[None]
    return (
        results_out,
        grad_out_in,
        attn_acc[0][None],
        attn_acc[1][None],
        mlp_acc[0][None],
        mlp_acc[1][None],
        attn_acc[2][None],
        mlp_acc[2][None],
        norm_sum[None],
    )


def solution(mesh):
    return jax.shard_map(
        local,
        mesh=mesh,
        in_specs=(
            P("section", "dp", "tensor", None),
            P("dp"),
            P("dp", None),
            P("dp", "tensor", None),
            P("section", None, None, "tensor"),
            P("section", "tensor", None),
            P("section", None, "tensor"),
            P("section", "tensor", None),
            P("section", None, "tensor"),
            P("section", "tensor"),
            P("section", None, None),
        ),
        out_specs=(
            P("section", "dp", "tensor", None),
            P("section", "dp", "tensor", None),
            P("section", None, None, "tensor"),
            P("section", "tensor", None),
            P("section", None, "tensor"),
            P("section", "tensor", None),
            P("section", None, "tensor"),
            P("section", "tensor"),
            P("section", None, None),
        ),
        check_vma=False,
    )
```

profile of v0, /device:TPU:0, one launch (start us, length us, event | category | flops | bytes accessed | tf_op | source)
XLA Modules:
  0.0 1116.6 jit_solution(6793303002397625045)
XLA Ops:
  48.3 25.8 %reduce-scatter.16.cloned.1.call-done = bf16[3,64,768]{2,1,0:T(8,128)(2,1)} async-done(((bf16[3,256,768]{2,1,0:T(8,128)(2,1)}), bf16[3,64,768]{2,1,0:T(8,128)(2,1)}) %reduce-scatter.16.cloned.1.call-update) | async-done | bytes 294928 | tf_op jit(solution)/shard_map/reduce_scatter | solution.py:87
  108.4 24.0 %reduce-scatter.18.cloned.1.call-done = bf16[3,64,768]{2,1,0:T(8,128)(2,1)} async-done(((bf16[3,256,768]{2,1,0:T(8,128)(2,1)}), bf16[3,64,768]{2,1,0:T(8,128)(2,1)}) %reduce-scatter.18.cloned.1.call-update) | async-done | bytes 294928 | tf_op jit(solution)/shard_map/reduce_scatter | solution.py:101
  187.7 25.8 %reduce-scatter.20.cloned.1.call-done = bf16[3,64,768]{2,1,0:T(8,128)(2,1)} async-done(((bf16[3,256,768]{2,1,0:T(8,128)(2,1)}), bf16[3,64,768]{2,1,0:T(8,128)(2,1)}) %reduce-scatter.20.cloned.1.call-update) | async-done | bytes 294928 | tf_op jit(solution)/shard_map/reduce_scatter | solution.py:87
  217.8 17.6 %all-gather.25.cloned.1.call-done = bf16[3,256,768]{2,1,0:T(8,128)(2,1)} async-done(((bf16[3,64,768]{2,1,0:T(8,128)(2,1)}), bf16[3,256,768]{2,1,0:T(8,128)(2,1)}) %all-gather.25.cloned.1.call-update) | async-done | bytes 1179664 | tf_op jit(solution)/shard_map/all_gather | solution.py:97
  248.3 25.2 %reduce-scatter.22.cloned.1.call-done = bf16[3,64,768]{2,1,0:T(8,128)(2,1)} async-done(((bf16[3,256,768]{2,1,0:T(8,128)(2,1)}), bf16[3,64,768]{2,1,0:T(8,128)(2,1)}) %reduce-scatter.22.cloned.1.call-update) | async-done | bytes 294928 | tf_op jit(solution)/shard_map/reduce_scatter | solution.py:101
  329.3 25.8 %reduce-scatter.24.cloned.1.call-done = bf16[3,64,768]{2,1,0:T(8,128)(2,1)} async-done(((bf16[3,256,768]{2,1,0:T(8,128)(2,1)}), bf16[3,64,768]{2,1,0:T(8,128)(2,1)}) %reduce-scatter.24.cloned.1.call-update) | async-done | bytes 294928 | tf_op jit(solution)/shard_map/reduce_scatter | solution.py:87
  359.3 17.6 %all-gather.31.cloned.1.call-done = bf16[3,256,768]{2,1,0:T(8,128)(2,1)} async-done(((bf16[3,64,768]{2,1,0:T(8,128)(2,1)}), bf16[3,256,768]{2,1,0:T(8,128)(2,1)}) %all-gather.31.cloned.1.call-update) | async-done | bytes 1179664 | tf_op jit(solution)/shard_map/all_gather | solution.py:97
  394.2 21.0 %reduce-scatter.26.cloned.1.call-done = bf16[3,64,768]{2,1,0:T(8,128)(2,1)} async-done(((bf16[3,256,768]{2,1,0:T(8,128)(2,1)}), bf16[3,64,768]{2,1,0:T(8,128)(2,1)}) %reduce-scatter.26.cloned.1.call-update) | async-done | bytes 294928 | tf_op jit(solution)/shard_map/reduce_scatter | solution.py:101
  418.0 17.6 %all-gather.33.cloned.1.call-done = bf16[3,256,768]{2,1,0:T(8,128)(2,1)} async-done(((bf16[3,64,768]{2,1,0:T(8,128)(2,1)}), bf16[3,256,768]{2,1,0:T(8,128)(2,1)}) %all-gather.33.cloned.1.call-update) | async-done | bytes 1179664 | tf_op jit(solution)/shard_map/all_gather | solution.py:153
  444.3 25.6 %reduce-scatter.28.cloned.1.call-done = bf16[3,64,768]{2,1,0:T(8,128)(2,1)} async-done(((bf16[3,256,768]{2,1,0:T(8,128)(2,1)}), bf16[3,64,768]{2,1,0:T(8,128)(2,1)}) %reduce-scatter.28.cloned.1.call-update) | async-done | bytes 294928 | tf_op jit(solution)/shard_map/reduce_scatter | solution.py:160
  477.5 17.6 %all-gather.35.cloned.1.call-done = bf16[3,256,768]{2,1,0:T(8,128)(2,1)} async-done(((bf16[3,64,768]{2,1,0:T(8,128)(2,1)}), bf16[3,256,768]{2,1,0:T(8,128)(2,1)}) %all-gather.35.cloned.1.call-update) | async-done | bytes 1179664 | tf_op jit(solution)/shard_map/all_gather | solution.py:199
  504.3 20.7 %fusion.93 = bf16[3,3,64,512]{3,2,1,0:T(8,128)(2,1)} fusion(bf16[3,256,3,64]{1,3,2,0:T(8,128)(2,1)} %bitcast.540, f32[3,3,256,512]{3,2,1,0:T(8,128)} %fusion.330, pred[3,256,512]{2,1,0:T(8,128)(4,1)} %get-tuple-element.121, f32[3,3,256,512]{3,2,1,0:T(8,128)} %get-tuple-element.146, f32[3,3,256]{2,1,0:T(4,128)} %get-tuple-element.145), kind=kOutput, calls=%fused_computation.166 | convolution fusion | flops 160729856 | bytes 10724352 | tf_op jit(solution)/shard_map/bhqk,bqhd->bkhd/dot_general | solution.py:224
  532.2 25.8 %reduce-scatter.32.cloned.1.call-done = bf16[3,64,768]{2,1,0:T(8,128)(2,1)} async-done(((bf16[3,256,768]{2,1,0:T(8,128)(2,1)}), bf16[3,64,768]{2,1,0:T(8,128)(2,1)}) %reduce-scatter.32.cloned.1.call-update) | async-done | bytes 294928 | tf_op jit(solution)/shard_map/reduce_scatter | solution.py:244
  603.5 25.4 %reduce-scatter.34.cloned.1.call-done = bf16[3,64,768]{2,1,0:T(8,128)(2,1)} async-done(((bf16[3,256,768]{2,1,0:T(8,128)(2,1)}), bf16[3,64,768]{2,1,0:T(8,128)(2,1)}) %reduce-scatter.34.cloned.1.call-update) | async-done | bytes 294928 | tf_op jit(solution)/shard_map/reduce_scatter | solution.py:160
  635.9 17.6 %all-gather.39.cloned.1.call-done = bf16[3,256,768]{2,1,0:T(8,128)(2,1)} async-done(((bf16[3,64,768]{2,1,0:T(8,128)(2,1)}), bf16[3,256,768]{2,1,0:T(8,128)(2,1)}) %all-gather.39.cloned.1.call-update) | async-done | bytes 1179664 | tf_op jit(solution)/shard_map/all_gather | solution.py:199
  662.9 20.9 %fusion.90 = bf16[3,3,64,512]{3,2,1,0:T(8,128)(2,1)} fusion(bf16[3,256,3,64]{1,3,2,0:T(8,128)(2,1)} %bitcast.538, f32[3,3,256,512]{3,2,1,0:T(8,128)} %fusion.331, pred[3,256,512]{2,1,0:T(8,128)(4,1)} %get-tuple-element.123, f32[3,3,256,512]{3,2,1,0:T(8,128)} %get-tuple-element.143, f32[3,3,256]{2,1,0:T(4,128)} %copy-done.184), kind=kOutput, calls=%fused_computation.165 | convolution fusion | flops 160729856 | bytes 10724352 | tf_op jit(solution)/shard_map/bhqk,bqhd->bkhd/dot_general | solution.py:224
  691.0 25.8 %reduce-scatter.38.cloned.1.call-done = bf16[3,64,768]{2,1,0:T(8,128)(2,1)} async-done(((bf16[3,256,768]{2,1,0:T(8,128)(2,1)}), bf16[3,64,768]{2,1,0:T(8,128)(2,1)}) %reduce-scatter.38.cloned.1.call-update) | async-done | bytes 294928 | tf_op jit(solution)/shard_map/reduce_scatter | solution.py:244
  763.3 25.6 %reduce-scatter.40.cloned.1.call-done = bf16[3,64,768]{2,1,0:T(8,128)(2,1)} async-done(((bf16[3,256,768]{2,1,0:T(8,128)(2,1)}), bf16[3,64,768]{2,1,0:T(8,128)(2,1)}) %reduce-scatter.40.cloned.1.call-update) | async-done | bytes 294928 | tf_op jit(solution)/shard_map/reduce_scatter | solution.py:160
  798.1 17.6 %all-gather.43.cloned.1.call-done = bf16[3,256,768]{2,1,0:T(8,128)(2,1)} async-done(((bf16[3,64,768]{2,1,0:T(8,128)(2,1)}), bf16[3,256,768]{2,1,0:T(8,128)(2,1)}) %all-gather.43.cloned.1.call-update) | async-done | bytes 1179664 | tf_op jit(solution)/shard_map/all_gather | solution.py:199
  825.1 17.6 %fusion.87 = bf16[3,3,64,512]{3,2,1,0:T(8,128)(2,1)} fusion(bf16[3,256,3,64]{1,3,2,0:T(8,128)(2,1)S(1)} %bitcast.536, f32[3,3,256,512]{3,2,1,0:T(8,128)} %fusion.332, pred[3,256,512]{2,1,0:T(8,128)(4,1)} %copy-done.81, f32[3,3,256,512]{3,2,1,0:T(8,128)} %get-tuple-element.140, f32[3,3,256]{2,1,0:T(4,128)} %copy-done.182), kind=kOutput, calls=%fused_computation.164 | convolution fusion | flops 160729856 | bytes 10724352 | tf_op jit(solution)/shard_map/bhqk,bqhd->bkhd/dot_general | solution.py:224
  880.3 17.6 %fusion.315 = (f32[3,64]{1,0:T(4,128)}, bf16[3,256,3,64]{1,3,2,0:T(8,128)(2,1)S(1)}) fusion(bf16[3,512,3,64]{1,3,2,0:T(8,128)(2,1)} %bitcast.532, f32[3,3,256,512]{3,2,1,0:T(8,128)} %fusion.331, pred[3,256,512]{2,1,0:T(8,128)(4,1)S(1)} %copy-done.82, f32[3,3,256,512]{3,2,1,0:T(8,128)} %get-tuple-element.143, f32[3,3,256]{2,1,0:T(4,128)S(1)} %copy-done.185), kind=kOutput, calls=%fused_computation.558 | convolution fusion | flops 160729664 | bytes 10725120 | tf_op jit(solution)/shard_map/bhqk,bkhd->bqhd/dot_general | solution.py:221
  915.8 17.9 %fusion.316 = (f32[3,64]{1,0:T(4,128)}, bf16[3,256,3,64]{1,3,2,0:T(8,128)(2,1)}) fusion(bf16[3,512,3,64]{1,3,2,0:T(8,128)(2,1)} %bitcast.530, f32[3,3,256,512]{3,2,1,0:T(8,128)} %fusion.332, pred[3,256,512]{2,1,0:T(8,128)(4,1)} %copy-done.81, f32[3,3,256,512]{3,2,1,0:T(8,128)} %get-tuple-element.140, f32[3,3,256]{2,1,0:T(4,128)} %copy-done.182), kind=kOutput, calls=%fused_computation.559 | convolution fusion | flops 160729664 | bytes 10725120 | tf_op jit(solution)/shard_map/bhqk,bkhd->bqhd/dot_general | solution.py:221
  974.6 61.6 %psum.55 = f32[1,8,768]{2,1,0:T(8,128)} all-reduce(f32[1,8,768]{2,1,0:T(8,128)S(1)} %add_bitcast_fusion), channel_id=1, replica_groups=mesh['section'=2,'dp'=4,'tensor'=4] {'dp','tensor'}, use_global_device_ids=true, to_apply=%region_101.102 | all-reduce | flops 6144 | bytes 49152 | tf_op jit(solution)/shard_map/psum | solution.py:375
  1043.8 57.8 %all-reduce.4.cloned.1.call-done = (bf16[1,3,768,192]{2,3,1,0:T(8,128)(2,1)}, bf16[1,192,768]{2,1,0:T(8,128)(2,1)}, bf16[1,768,768]{2,1,0:T(8,128)(2,1)}, bf16[1,768,768]{2,1,0:T(8,128)(2,1)}) async-done(((bf16[1,3,768,192]{2,3,1,0:T(8,128)(2,1)}, bf16[1,192,768]{2,1,0:T(8,128)(2,1)}, bf16[1,768,768]{2,1,0:T(8,128)(2,1)}, bf16[1,768,768]{2,1,0:T(8,128)(2,1)}), (bf16[1,3,768,192]{2,3,1,0:T(8,128)(2,1)}, ...) | async-done | bytes 3538960 | tf_op jit(solution)/shard_map/psum | solution.py:366
  (686 shorter events, 503.7 us)
Async XLA Ops:
  12.1 62.0 %reduce-scatter.16.cloned.1.call-start = ((), (), s32[]{:S(2)}) async-start(), calls=%async_computation.16 | async-start | bytes 1474560 | tf_op jit(solution)/shard_map/reduce_scatter | solution.py:87
  76.4 55.9 %reduce-scatter.18.cloned.1.call-start = ((), (), s32[]{:S(2)}) async-start(), calls=%async_computation.18 | async-start | bytes 1474560 | tf_op jit(solution)/shard_map/reduce_scatter | solution.py:101
  107.0 64.2 %all-gather.21.cloned.1.call-start = ((), (), s32[]{:S(2)}) async-start(), calls=%async_computation.19 | async-start | bytes 1474560 | tf_op jit(solution)/shard_map/all_gather | solution.py:52
  145.4 68.1 %reduce-scatter.20.cloned.1.call-start = ((), (), s32[]{:S(2)}) async-start(), calls=%async_computation.21 | async-start | bytes 1474560 | tf_op jit(solution)/shard_map/reduce_scatter | solution.py:87
  217.7 55.9 %reduce-scatter.22.cloned.1.call-start = ((), (), s32[]{:S(2)}) async-start(), calls=%async_computation.23 | async-start | bytes 1474560 | tf_op jit(solution)/shard_map/reduce_scatter | solution.py:101
  248.3 63.8 %all-gather.27.cloned.1.call-start = ((), (), s32[]{:S(2)}) async-start(), calls=%async_computation.24 | async-start | bytes 1474560 | tf_op jit(solution)/shard_map/all_gather | solution.py:52
  287.5 67.6 %reduce-scatter.24.cloned.1.call-start = ((), (), s32[]{:S(2)}) async-start(), calls=%async_computation.26 | async-start | bytes 1474560 | tf_op jit(solution)/shard_map/reduce_scatter | solution.py:87
  329.2 47.6 %all-gather.31.cloned.1.call-start = ((), (), s32[]{:S(2)}) async-start(), calls=%async_computation.27 | async-start | bytes 1474560 | tf_op jit(solution)/shard_map/all_gather | solution.py:97
  359.2 55.9 %reduce-scatter.26.cloned.1.call-start = ((), (), s32[]{:S(2)}) async-start(), calls=%async_computation.28 | async-start | bytes 1474560 | tf_op jit(solution)/shard_map/reduce_scatter | solution.py:101
  417.9 52.1 %reduce-scatter.28.cloned.1.call-start = ((), (), s32[]{:S(2)}) async-start(), calls=%async_computation.30 | async-start | bytes 1474560 | tf_op jit(solution)/shard_map/reduce_scatter | solution.py:160
  444.1 50.9 %all-gather.35.cloned.1.call-start = ((), (), s32[]{:S(2)}) async-start(), calls=%async_computation.31 | async-start | bytes 1474560 | tf_op jit(solution)/shard_map/all_gather | solution.py:199
  477.4 80.6 %reduce-scatter.32.cloned.1.call-start = ((), (), s32[]{:S(2)}) async-start(), calls=%async_computation.33 | async-start | bytes 1474560 | tf_op jit(solution)/shard_map/reduce_scatter | solution.py:244
  532.2 62.2 %all-gather.37.cloned.1.call-start = ((), (), s32[]{:S(2)}) async-start(), calls=%async_computation.34 | async-start | bytes 1474560 | tf_op jit(solution)/shard_map/all_gather | solution.py:153
  577.7 51.2 %reduce-scatter.34.cloned.1.call-start = ((), (), s32[]{:S(2)}) async-start(), calls=%async_computation.35 | async-start | bytes 1474560 | tf_op jit(solution)/shard_map/reduce_scatter | solution.py:160
  603.0 50.5 %all-gather.39.cloned.1.call-start = ((), (), s32[]{:S(2)}) async-start(), calls=%async_computation.36 | async-start | bytes 1474560 | tf_op jit(solution)/shard_map/all_gather | solution.py:199
  635.9 81.0 %reduce-scatter.38.cloned.1.call-start = ((), (), s32[]{:S(2)}) async-start(), calls=%async_computation.38 | async-start | bytes 1474560 | tf_op jit(solution)/shard_map/reduce_scatter | solution.py:244
  691.0 63.6 %all-gather.41.cloned.1.call-start = ((), (), s32[]{:S(2)}) async-start(), calls=%async_computation.39 | async-start | bytes 1474560 | tf_op jit(solution)/shard_map/all_gather | solution.py:153
  737.8 51.1 %reduce-scatter.40.cloned.1.call-start = ((), (), s32[]{:S(2)}) async-start(), calls=%async_computation.40 | async-start | bytes 1474560 | tf_op jit(solution)/shard_map/reduce_scatter | solution.py:160
  763.1 52.6 %all-gather.43.cloned.1.call-start = ((), (), s32[]{:S(2)}) async-start(), calls=%async_computation.41 | async-start | bytes 1474560 | tf_op jit(solution)/shard_map/all_gather | solution.py:199
  798.1 171.6 %reduce-scatter.44.cloned.1.call-start = ((), (), s32[]{:S(2)}) async-start(), calls=%async_computation.43 | async-start | bytes 1474560 | tf_op jit(solution)/shard_map/reduce_scatter | solution.py:244
  848.9 121.9 %reduce-scatter.30.cloned.1.call-start = ((), (), s32[]{:S(2)}) async-start(), calls=%async_computation.32 | async-start | bytes 1474560 | tf_op jit(solution)/shard_map/reduce_scatter | solution.py:241
  869.7 101.1 %reduce-scatter.36.cloned.1.call-start = ((), (), s32[]{:S(2)}) async-start(), calls=%async_computation.37 | async-start | bytes 1474560 | tf_op jit(solution)/shard_map/reduce_scatter | solution.py:241
  901.4 69.4 %reduce-scatter.42.cloned.1.call-start = ((), (), s32[]{:S(2)}) async-start(), calls=%async_computation.42 | async-start | bytes 1474560 | tf_op jit(solution)/shard_map/reduce_scatter | solution.py:241
  937.1 164.5 %all-reduce.4.cloned.1.call-start = ((), (), s32[]{:S(2)}) async-start(), calls=%async_computation.44 | async-start | bytes 7077888 | tf_op jit(solution)/shard_map/psum | solution.py:366
  (196 other events, 1795.1 us)
Sparse Core Ops, SparseCore 0:
  12.2 20.1 all-gather.16
  48.3 25.7 reduce-scatter.15
  76.5 17.4 all-gather.18
  106.6 25.7 reduce-scatter.17
  153.8 17.4 all-gather.20
  187.8 25.7 reduce-scatter.19
  217.8 17.4 all-gather.24
  247.8 25.7 reduce-scatter.21
  275.0 17.4 all-gather.28
  329.3 25.7 reduce-scatter.23
  359.4 17.4 all-gather.30
  389.4 25.7 reduce-scatter.25
  444.2 25.7 reduce-scatter.27
  477.5 17.4 all-gather.34
  532.3 25.7 reduce-scatter.31
  603.1 25.7 reduce-scatter.33
  691.1 25.7 reduce-scatter.37
  763.2 25.7 reduce-scatter.39
  798.2 17.4 all-gather.42
  849.0 25.8 reduce-scatter.43
  877.3 25.7 reduce-scatter.29
  905.9 25.7 reduce-scatter.35
  937.2 25.6 reduce-scatter.41
  966.2 135.3 all-reduce.3
  (6 shorter events, 102.6 us)
where the time goes:
time: 1130 us; the launch traced here: 1120 us
  waiting for transfers between devices  580 us (51%)
  matrix products  279 us (25%)
  other arithmetic  109 us (10%)
  blocking collectives  79.7 us (7%)
  local copies, waits for them, and re-layouts  39.3 us (3%)
  between operations  17.3 us (2%)
  starting transfers between devices  12.2 us (1%)
    reduce_scatter x3, waiting for transfers between devices, forward_block(): lax.psum_scatter(rows_product(mixed_low, w_out).astype(jnp.bfloat16), 'te...  77.5 us
    reduce_scatter x3, waiting for transfers between devices, mlp_back(): lax.psum_scatter(rows_transposed(pre_low, w_up).astype(jnp.bfloat16), 'te...  76.7 us
    reduce_scatter x3, waiting for transfers between devices, forward_block(): lax.psum_scatter(rows_product(hidden, w_down).astype(jnp.bfloat16), 'tens...  70.2 us
    psum x1, blocking collectives, local(): norm_sum = lax.psum(norm_acc, ('dp', 'tensor'))  61.6 us
    dot_general x3, matrix products, attn_back(): jnp.einsum('bhqk,bqhd->bkhd', d_raw, queries, preferred_element_type=jnp....  59.2 us
    psum x1, waiting for transfers between devices, local(): lax.psum(attn_acc[0].astype(jnp.bfloat16), 'dp').astype(jnp.float32)  57.8 us
    dot_general x3, matrix products, attn_back(): jnp.einsum('bhqk,bkhd->bqhd', d_raw, keys_low, preferred_element_type=jnp...  53 us
    all_gather x3, waiting for transfers between devices, attn_back(): lax.all_gather(d_attended.astype(jnp.bfloat16), 'tensor', axis=1, tiled=T...  52.7 us
  transfers between devices with their start and end apart: 34, of which 30 were waited for; matrix products, arithmetic and copies ran while one was open for 12% of the time, Pallas kernels for 0%

commit v1 on v0

v1 whole, which is shorter than its diff:
```python
import functools

import jax
import jax.numpy as jnp
from jax import lax
from jax.experimental import pallas as pl
from jax.experimental.pallas import tpu as pltpu
from jax.sharding import PartitionSpec as P

HD = 64
CH = 128
EPS = 1e-06
MASKED = -1000000000.0
F32 = jnp.float32
BF16 = jnp.bfloat16


class Places:
    def __init__(self):
        self.count = 0

    def take(self, many=1):
        first = self.count
        self.count += many
        return first


def nn(a, b):
    return lax.dot_general(a, b, (((1,), (0,)), ((), ())), preferred_element_type=F32)


def nt(a, b):
    return lax.dot_general(a, b, (((1,), (1,)), ((), ())), preferred_element_type=F32)


def tn(a, b):
    return lax.dot_general(a, b, (((0,), (0,)), ((), ())), preferred_element_type=F32)


def normal(u):
    mean = jnp.mean(u, axis=-1, keepdims=True)
    centred = u - mean
    spread = jnp.mean(centred * centred, axis=-1, keepdims=True)
    inverse = lax.rsqrt(spread + EPS)
    return centred * inverse, inverse


def normal_back(hat, inverse, grad):
    first = jnp.mean(grad, axis=-1, keepdims=True)
    second = jnp.mean(grad * hat, axis=-1, keepdims=True)
    return inverse * (grad - first - hat * second)


def column_sum(u):
    return jnp.sum(u, axis=0, keepdims=True)


class Sizes:
    def __init__(self, n_dp, images, slots, width, piece):
        self.n_dp = n_dp
        self.images = images
        self.slots = slots
        self.width = width
        self.piece = piece
        self.block = 2 * slots
        self.rows = images * self.block
        self.pair = 2 * piece
        self.heads = self.pair // HD
        self.parts = 3 * width // CH


def plan(z):
    p = Places()
    half = z.width // 2 // CH
    s = dict(
        x=p.take(), bias=p.take(), xc0=p.take(), xc1=p.take(), pg=p.take(),
        wy=p.take(3 * half), wz=p.take(3 * half),
        e=p.take(z.images), ec=p.take(z.images),
        attn=p.take(), h2=p.take(), br=p.take(), dbl=p.take(), dh2=p.take(), dal=p.take(), dn=p.take(),
        dlat=p.take(z.images), res=p.take(), gin=p.take(),
        gy=p.take(z.parts), ga=p.take(z.parts), gb=p.take(z.parts),
        sy=p.take(), sc=p.take(), sa=p.take(), sb=p.take(),
    )
    return s, p.count


def body(
    z, S,
    x_ref, pg_ref, wa_ref, wu_ref, wd_ref, bias_ref, norm_ref, col_ref, key_ref,
    res_ref, gin_ref, grad_ref, small_ref,
    wy, xall, pgr, br_bias, e_own, e_oth, h, kv, q, kk, vv, o, p, att, mid, h2, act, gp, brv, dy,
    snd, rcv, dbl, dal, dol, dq, dk, dv, g, yr, za, zb, dlat, outb, nacc, sml, small_in,
    ss, rs, ls,
):
    sec = lax.axis_index("section")
    dp = lax.axis_index("dp")
    t = lax.axis_index("tensor")
    y = t // 2
    c = t % 2
    to_y = {"tensor": 2 * (1 - y) + c}
    to_c = {"tensor": 2 * y + 1 - c}
    to_s = {"section": 1 - sec}
    pair_z = {"dp": dp + 1 - 2 * (dp % 2)}
    top = dp // (z.n_dp // 2)
    to_m = {"dp": dp + 1 - 2 * top}
    to_w = {"dp": dp - 1 + 2 * top}
    is_end = jnp.logical_or(dp == 0, dp == z.n_dp - 1)
    not_end = jnp.logical_not(is_end)
    is_mid = jnp.logical_or(dp == z.n_dp // 2 - 1, dp == z.n_dp // 2)
    not_mid = jnp.logical_not(is_mid)
    enc = sec == 0
    reg = sec == 1

    I, R, D, BL, SL = z.images, z.rows, z.width, z.block, z.slots
    PC, PW = z.piece, z.pair
    HALF = D // 2
    NH = HALF // CH
    KEYS = 2 * BL

    def far(src, dst, number, to, receive=None):
        return pltpu.make_async_remote_copy(
            src_ref=src, dst_ref=dst, send_sem=ss.at[number],
            recv_sem=rs.at[number if receive is None else receive],
            device_id=to, device_id_type=pl.DeviceIdType.MESH,
        )

    barrier = pltpu.get_barrier_semaphore()

    def greet(to):
        pl.semaphore_signal(barrier, inc=1, device_id=to, device_id_type=pl.DeviceIdType.MESH)

    greet(to_y)
    greet(to_c)
    greet(to_s)
    greet(to_m)

    @pl.when(not_end)
    def _():
        greet(to_w)
        pl.semaphore_wait(barrier, 5)

    @pl.when(is_end)
    def _():
        pl.semaphore_wait(barrier, 4)

    c_x = far(x_ref.at[1 - y], xall.at[0, :, 1], S["x"], to_y)
    c_x.start()
    c_bias = far(bias_ref, br_bias, S["bias"], to_y)
    c_bias.start()
    c_xc0 = far(x_ref.at[y], xall.at[1, :, 0], S["xc0"], to_c)
    c_xc0.start()
    own_w = (wa_ref, wu_ref, wd_ref)
    parity = dp % 2

    def rows_of(m, k, mine):
        which = parity if mine else 1 - parity
        return pl.ds(pl.multiple_of(which * HALF + k * CH, CH), CH)

    def w_y(m, k):
        at = rows_of(m, k, True)
        return far(own_w[m].at[at], wy.at[m, at], S["wy"] + m * NH + k, to_y)

    def w_z(m, k):
        at = rows_of(m, k, True)
        return far(wy.at[m, at], wy.at[m, at], S["wz"] + m * NH + k, pair_z)

    for m in range(3):
        for k in range(NH):
            w_y(m, k).start()
    c_pg = far(pg_ref.at[1 - y], pgr, S["pg"], to_y)
    c_pg.start()

    def forward_w(m):
        for k in range(NH):
            w_y(m, k).wait_recv()
            w_z(m, k).start()

    def finish_w(m):
        for k in range(NH):
            w_z(m, k).wait_recv()

    g0, b0 = norm_ref[0:1, :], norm_ref[1:2, :]

    def lay(block):
        return block.reshape(BL, D)

    xall[0, :, 0] = x_ref[y]
    c_x.wait_recv()
    c_xc1 = far(xall.at[0, :, 1], xall.at[1, :, 1], S["xc1"], to_c)
    c_xc1.start()

    def norm_rows(half):
        def one(i, carry):
            hat, _ = normal(lay(xall[half, i]).astype(F32))
            value = (hat * g0 + b0).astype(BF16)
            h[half, i] = value
            kv[half, i] = value
            return carry

        lax.fori_loop(0, I, one, 0)

    norm_rows(0)
    c_xc0.wait_recv()
    c_xc1.wait_recv()
    norm_rows(1)
    forward_w(0)
    c_bias.wait_recv()
    finish_w(0)
    forward_w(1)
    forward_w(2)

    def both_rows(first, many):
        return jnp.concatenate([wa_ref[first:first + many], wy[0, first:first + many]], axis=0)

    bq = bias_ref[0:1, 0:PW] + br_bias[1:2, 0:PW]
    bv = bias_ref[2:3, 0:PW] + br_bias[3:4, 0:PW]

    def flat(ref, half):
        return ref[half].reshape(R, ref.shape[-1])

    def e_hop(i):
        return far(dlat.at[0, i], e_own.at[i], S["e"] + i, to_s)

    def e_core(i):
        return far(e_own.at[i], e_oth.at[i], S["ec"] + i, to_c)

    @pl.when(reg)
    def _():
        def take(half, ref, i):
            hat, _ = normal(ref[i].astype(F32))
            value = (hat * g0 + b0).astype(BF16)
            seen = col_ref[half, i][:, 1:2] > 0.5
            kv[half, i] = jnp.where(seen, value, h[half, i])

        for i in range(I):
            e_hop(i).wait_recv()
            e_core(i).start()
            take(0, e_own, i)
        for i in range(I):
            e_core(i).wait_recv()
            take(1, e_oth, i)

    for half in range(2):
        rows_h = flat(h, half)
        rows_k = flat(kv, half)
        q[half] = ((nt(rows_h, both_rows(0, PC)) + bq).astype(BF16) * 0.125).reshape(I, BL, PW)
        kk[half] = nt(rows_k, both_rows(PC, PC)).astype(BF16).reshape(I, BL, PW)
        vv[half] = (nt(rows_k, both_rows(2 * PC, PC)) + bv).astype(BF16).reshape(I, BL, PW)

    lane = lax.broadcasted_iota(jnp.int32, (KEYS, 2 * HD), 1)
    lanes = (lane < HD, lane >= HD)
    zero16 = jnp.zeros((KEYS, 2 * HD), BF16)

    def image(ref, i, pr):
        at = slice(pr * 2 * HD, (pr + 1) * 2 * HD)
        return jnp.concatenate([ref[0, i, :, at], ref[1, i, :, at]], axis=0)

    def put(ref, i, pr, value):
        at = slice(pr * 2 * HD, (pr + 1) * 2 * HD)
        ref[0, i, :, at] = value[:BL]
        ref[1, i, :, at] = value[BL:]

    def attend(i, carry):
        codes = jnp.concatenate([col_ref[0, i][:, 0:1], col_ref[1, i][:, 0:1]], axis=0)
        shut = jnp.where(codes == key_ref[i], 0.0, MASKED)
        for pr in range(z.heads // 2):
            qp, kp, vp = image(q, i, pr), image(kk, i, pr), image(vv, i, pr)
            outs = []
            for sub in range(2):
                scores = nt(jnp.where(lanes[sub], qp, zero16), kp) + shut
                top_value = jnp.max(scores, axis=-1, keepdims=True)
                e = jnp.exp(scores - top_value)
                probs = (e * (1.0 / jnp.sum(e, axis=-1, keepdims=True))).astype(BF16)
                p[i, 2 * pr + sub] = probs
                outs.append(nn(probs, vp))
            put(o, i, pr, jnp.where(lanes[0], outs[0], outs[1]).astype(BF16))
        return carry

    lax.fori_loop(0, I, attend, 0)

    w_o = both_rows(3 * PC, PC)

    def exchange(slot, buffer, number):
        return far(snd.at[buffer], rcv.at[slot], number, to_c)

    snd[0] = nn(flat(o, 1), w_o).astype(BF16).reshape(I, BL, D)
    c_attn = exchange(0, 0, S["attn"])
    c_attn.start()
    att[...] = nn(flat(o, 0), w_o).reshape(I, BL, D)
    c_attn.wait_recv()

    def middle(i, carry):
        attn = att[i] + rcv[0, i].astype(F32) + norm_ref[2:3, :]
        att[i] = attn
        value = lay(xall[0, i]).astype(F32) + norm_ref[3:4, :] * attn
        mid[i] = value
        hat, _ = normal(value)
        h2[0, i] = (hat * norm_ref[4:5, :] + norm_ref[5:6, :]).astype(BF16)
        return carry

    lax.fori_loop(0, I, middle, 0)
    c_h2 = far(h2.at[0], h2.at[1], S["h2"], to_c)
    c_h2.start()

    TW = 256
    NT = D // TW

    def up(half, w, w_ref, b_row):
        rows2 = flat(h2, half)

        def one(n, carry):
            at = pl.ds(pl.multiple_of(n * TW, TW), TW)
            u = nn(rows2, w_ref[:, at]) + b_row[:, at]
            cdf = 0.5 + 0.5 * lax.erf(u * 0.7071067811865476)
            act[w, half, :, at] = (u * cdf).astype(BF16)
            gp[w, half, :, at] = (cdf + u * (0.3989422804014327 * jnp.exp(-0.5 * u * u))).astype(BF16)
            return carry

        lax.fori_loop(0, NT, one, 0)

    up(0, 0, wu_ref, bias_ref.at[4:5])
    c_h2.wait_recv()
    up(1, 0, wu_ref, bias_ref.at[4:5])
    finish_w(1)
    up(0, 1, wy.at[1], br_bias.at[4:5])
    up(1, 1, wy.at[1], br_bias.at[4:5])
    finish_w(2)

    def down(half):
        rows0, rows1 = act[0, half], act[1, half]
        return nn(rows0, wd_ref[...]) + nn(rows1, wy[2])

    snd[1] = down(1).astype(BF16).reshape(I, BL, D)
    c_br = exchange(1, 1, S["br"])
    c_br.start()
    brv[...] = down(0).reshape(I, BL, D)
    c_br.wait_recv()

    def finish(i):
        br = brv[i] + rcv[1, i].astype(F32) + norm_ref[6:7, :]
        brv[i] = br
        out = mid[i] + norm_ref[7:8, :] * br
        dlat[0, i] = (out * col_ref[0, i][:, 1:2]).astype(BF16)

        @pl.when(enc)
        def _():
            e_hop(i).start()

        outb[0, i] = (out * col_ref[0, i][:, 2:3]).astype(BF16).reshape(2, SL, D)

    for i in range(I):
        finish(i)

    def deliver(which, number, ref):
        return (
            pltpu.make_async_copy(outb.at[which, :, 0], ref.at[y], ls.at[z.parts + which]),
            far(outb.at[which, :, 1], ref.at[y], S[number], to_y),
        )

    for copy in deliver(0, "res", res_ref):
        copy.start()

    nacc[...] = jnp.zeros_like(nacc)

    def add_norm(row, value):
        nacc[row:row + 1, :] += value

    def d_hop(i):
        return far(dlat.at[0, i], dlat.at[1, i], S["dlat"] + i, to_s)

    c_pg.wait_recv()

    def start_back(i, carry):
        grad = dy[i]
        add_norm(7, column_sum(grad * brv[i]))
        d_branch = norm_ref[7:8, :] * grad
        add_norm(6, column_sum(d_branch))
        dbl[0, i] = d_branch.astype(BF16)
        return carry

    @pl.when(reg)
    def _():
        for i in range(I):
            dy[i] = jnp.concatenate([pg_ref[y, i], pgr[i]], axis=0).astype(F32) * col_ref[0, i][:, 2:3]

    @pl.when(enc)
    def _():
        for i in range(I):
            d_hop(i).wait_recv()
            dy[i] = dlat[1, i].astype(F32) * col_ref[0, i][:, 1:2]

    lax.fori_loop(0, I, start_back, 0)
    c_dbl = far(dbl.at[0], dbl.at[1], S["dbl"], to_c)
    c_dbl.start()

    small_in[...] = jnp.zeros_like(small_in)

    def down_back(half, w, w_ref):
        rows = flat(dbl, half)

        def one(n, carry):
            at = pl.ds(pl.multiple_of(n * TW, TW), TW)
            du = nt(rows, w_ref[at, :]) * gp[w, half, :, at].astype(F32)
            small_in[8 + w:9 + w, at] += column_sum(du)
            gp[w, half, :, at] = du.astype(BF16)
            return carry

        lax.fori_loop(0, NT, one, 0)

    def y_part(k):
        at = pl.ds(pl.multiple_of(k * CH, CH), CH)
        return far(g.at[1, at], yr.at[at], S["gy"] + k, to_y)

    first_down, first_up, first_attn = 0, D // CH, 2 * D // CH

    def outer_rows(left, right, w, first, tile):
        def one(n, carry):
            at = pl.ds(pl.multiple_of(n * tile, tile), tile)
            to = pl.ds(pl.multiple_of(first * CH + n * tile, tile), tile)
            g[w, to, :] = tn(left(at), right()).astype(BF16)
            return carry

        lax.fori_loop(0, D // tile, one, 0)

    def wide(ref, w):
        return lambda at: ref[w, :, :, at].reshape(2 * R, at.size)

    down_back(0, 1, wy.at[2])
    down_back(0, 0, wd_ref)
    c_dbl.wait_recv()
    outer_rows(wide(act, 1), lambda: dbl[...].reshape(2 * R, D), 1, first_down, TW)
    for k in range(first_down, first_up):
        y_part(k).start()
    down_back(1, 1, wy.at[2])
    down_back(1, 0, wd_ref)

    def up_back(half):
        return nt(gp[0, half], wu_ref[...]) + nt(gp[1, half], wy[1])

    c_attn.wait_send()
    snd[0] = up_back(1).astype(BF16).reshape(I, BL, D)
    c_dh2 = exchange(2, 0, S["dh2"])
    c_dh2.start()

    def h2_cols(at):
        return jnp.concatenate(
            [h2[0, :, :, at].reshape(R, at.size), h2[1, :, :, at].reshape(R, at.size)], axis=0
        )

    outer_rows(h2_cols, lambda: gp[1].reshape(2 * R, D), 1, first_up, TW)
    for k in range(first_up, first_attn):
        y_part(k).start()
    back0 = up_back(0).reshape(I, BL, D)
    c_dh2.wait_recv()

    att_rows = []
    for i in range(I):
        grad = back0[i] + rcv[2, i].astype(F32)
        hat, inverse = normal(mid[i])
        add_norm(4, column_sum(grad * hat))
        add_norm(5, column_sum(grad))
        d_mid = dy[i] + normal_back(hat, inverse, grad * norm_ref[4:5, :])
        dy[i] = d_mid
        add_norm(3, column_sum(d_mid * att[i]))
        d_att = norm_ref[3:4, :] * d_mid
        add_norm(2, column_sum(d_att))
        dal[0, i] = d_att.astype(BF16)
    c_dal = far(dal.at[0], dal.at[1], S["dal"], to_c)
    c_dal.start()
    outer_rows(wide(act, 0), lambda: dbl[...].reshape(2 * R, D), 0, first_down, TW)
    outer_rows(h2_cols, lambda: gp[0].reshape(2 * R, D), 0, first_up, TW)

    dol[0] = nt(flat(dal, 0), w_o).astype(BF16).reshape(I, BL, PW)
    c_dal.wait_recv()
    dol[1] = nt(flat(dal, 1), w_o).astype(BF16).reshape(I, BL, PW)

    def all_rows(ref):
        return ref[...].reshape(2 * R, ref.shape[-1])

    base = first_attn * CH

    def store_rows(value, first):
        g[0, base + first:base + first + PC, :] = value[:PC].astype(BF16)
        g[1, base + first:base + first + PC, :] = value[PC:].astype(BF16)

    def attend_back(i, carry):
        for pr in range(z.heads // 2):
            qp, kp, vp, gpair = image(q, i, pr), image(kk, i, pr), image(vv, i, pr), image(dol, i, pr)
            at = slice(pr * 2 * HD, (pr + 1) * 2 * HD)
            dqs, dks, dvs = [], [], []
            for sub in range(2):
                probs = p[i, 2 * pr + sub]
                wide_probs = probs.astype(F32)
                d_probs = nt(jnp.where(lanes[sub], gpair, zero16), vp)
                dvs.append(tn(probs, gpair))
                inner = jnp.sum(d_probs * wide_probs, axis=-1, keepdims=True)
                ds = (wide_probs * (d_probs - inner)).astype(BF16)
                dqs.append(nn(ds, kp))
                dks.append(tn(ds, qp))
            d_q = jnp.where(lanes[0], dqs[0], dqs[1]) * 0.125
            d_k = jnp.where(lanes[0], dks[0], dks[1])
            d_v = jnp.where(lanes[0], dvs[0], dvs[1])
            small_in[10:11, at] += column_sum(d_q)
            small_in[11:12, at] += column_sum(d_v)
            put(dq, i, pr, d_q.astype(BF16))
            put(dk, i, pr, d_k.astype(BF16))
            put(dv, i, pr, d_v.astype(BF16))
        return carry

    lax.fori_loop(0, I, attend_back, 0)

    def input_back(half):
        return (
            nn(flat(dq, half), both_rows(0, PC))
            + nn(flat(dk, half), both_rows(PC, PC))
            + nn(flat(dv, half), both_rows(2 * PC, PC))
        )

    c_br.wait_send()
    snd[1] = input_back(1).astype(BF16).reshape(I, BL, D)
    c_dn = exchange(3, 1, S["dn"])
    c_dn.start()
    back1 = input_back(0).reshape(I, BL, D)
    c_dn.wait_recv()
    for i in range(I):
        grad = back1[i] + rcv[3, i].astype(F32)
        seen = col_ref[0, i][:, 1:2]
        extra = jnp.logical_and(seen > 0.5, reg)
        own = jnp.where(extra, 0.0, grad)
        hat, inverse = normal(lay(xall[0, i]).astype(F32))
        add_norm(0, column_sum(own * hat))
        add_norm(1, column_sum(own))
        d_x = dy[i] + normal_back(hat, inverse, own * g0)
        outb[1, i] = d_x.astype(BF16).reshape(2, SL, D)

        @pl.when(reg)
        def _():
            other = jnp.where(extra, grad, 0.0)
            hat, inverse = normal(e_own[i].astype(F32))
            add_norm(0, column_sum(other * hat))
            add_norm(1, column_sum(other))
            dlat[0, i] = normal_back(hat, inverse, other * g0).astype(BF16)
            d_hop(i).start()

    store_rows(tn(all_rows(dq), all_rows(h)), 0)
    store_rows(tn(all_rows(dk), all_rows(kv)), PC)
    store_rows(tn(all_rows(dv), all_rows(kv)), 2 * PC)
    store_rows(tn(all_rows(o), all_rows(dal)), 3 * PC)
    for k in range(first_attn, z.parts):
        y_part(k).start()
    for copy in deliver(1, "gin", gin_ref):
        copy.start()

    small_in[0:8, :] = nacc[...]
    c_sy = far(small_in, sml.at[0], S["sy"], to_y)
    c_sy.start()

    def part(k):
        return pl.ds(pl.multiple_of(k * CH, CH), CH)

    def to_middle(k, start):
        at = part(k)

        @pl.when(is_mid)
        def _():
            copy = far(g.at[0, at], zb.at[at], S["ga"] + k, to_m, S["gb"] + k)
            copy.start() if start else copy.wait_send()

        @pl.when(not_mid)
        def _():
            copy = far(g.at[0, at], za.at[at], S["ga"] + k, to_m)
            copy.start() if start else copy.wait_send()

    def from_away(k):
        at = part(k)
        return far(g.at[0, at], za.at[at], S["ga"] + k, to_w)

    def total(k):
        at = part(k)
        return far(zb.at[at], zb.at[at], S["gb"] + k, to_w)

    def stage0(k):
        at = part(k)
        y_part(k).wait_recv()
        g[0, at, :] = (g[0, at, :].astype(F32) + yr[at, :].astype(F32)).astype(BF16)

        @pl.when(is_end)
        def _():
            to_middle(k, True)

    def stage1(k):
        at = part(k)

        @pl.when(not_end)
        def _():
            from_away(k).wait_recv()
            g[0, at, :] = (g[0, at, :].astype(F32) + za[at, :].astype(F32)).astype(BF16)
            to_middle(k, True)

    def stage2(k):
        at = part(k)
        total(k).wait_recv()

        @pl.when(is_mid)
        def _():
            zb[at, :] = (g[0, at, :].astype(F32) + zb[at, :].astype(F32)).astype(BF16)

        @pl.when(not_end)
        def _():
            total(k).start()

        pltpu.make_async_copy(zb.at[at], grad_ref.at[at], ls.at[k]).start()

    N = z.parts

    def step(k, carry):
        @pl.when(k < N)
        def _():
            stage0(k)

        @pl.when(jnp.logical_and(k >= 1, k < N + 1))
        def _():
            stage1(k - 1)

        @pl.when(jnp.logical_and(is_mid, jnp.logical_and(k >= 2, k < N + 2)))
        def _():
            stage2(k - 2)

        @pl.when(jnp.logical_and(not_mid, k >= 4))
        def _():
            stage2(k - 4)

        return carry

    lax.fori_loop(0, N + 4, step, 0)

    c_sy.wait_recv()
    sml[1, 0:8, :] = small_in[0:8, :] + sml[0, 0:8, :]
    sml[1, 8:9, :] = small_in[8:9, :] + sml[0, 9:10, :]
    sml[1, 9:10, :] = jnp.zeros((1, D), F32)
    sml[1, 10:12, :] = small_in[10:12, :]
    sml[1, 12:14, :] = sml[0, 10:12, :]
    sml[1, 14:16, :] = jnp.zeros((2, D), F32)
    c_sc = far(sml.at[1], sml.at[2], S["sc"], to_c)
    c_sc.start()
    c_sc.wait()
    sml[1, 0:8, :] = sml[1, 0:8, :] + sml[2, 0:8, :]

    def small_middle(start):
        @pl.when(is_mid)
        def _():
            copy = far(sml.at[1], sml.at[4], S["sa"], to_m, S["sb"])
            copy.start() if start else copy.wait_send()

        @pl.when(not_mid)
        def _():
            copy = far(sml.at[1], sml.at[3], S["sa"], to_m)
            copy.start() if start else copy.wait_send()

    @pl.when(not_end)
    def _():
        far(sml.at[1], sml.at[3], S["sa"], to_w).wait_recv()
        sml[1] = sml[1] + sml[3]

    small_middle(True)
    s_total = far(sml.at[4], sml.at[4], S["sb"], to_w)
    s_total.wait_recv()

    @pl.when(is_mid)
    def _():
        sml[4] = sml[1] + sml[4]

    @pl.when(not_end)
    def _():
        s_total.start()

    small_ref[...] = sml[4]

    small_middle(False)

    @pl.when(not_end)
    def _():
        s_total.wait_send()

    c_sy.wait_send()

    def end_parts(k, carry):
        y_part(k).wait_send()
        to_middle(k, False)

        @pl.when(not_end)
        def _():
            total(k).wait_send()

        pltpu.make_async_copy(zb.at[part(k)], grad_ref.at[part(k)], ls.at[k]).wait()
        return carry

    lax.fori_loop(0, N, end_parts, 0)
    for which, number, ref in ((0, "res", res_ref), (1, "gin", gin_ref)):
        for copy in deliver(which, number, ref):
            copy.wait()
    for copy in (c_x, c_bias, c_xc0, c_xc1, c_pg, c_h2, c_dbl, c_dh2, c_dal, c_dn):
        copy.wait_send()
    for m in range(3):
        for k in range(NH):
            w_y(m, k).wait_send()
            w_z(m, k).wait_send()
    for i in range(I):
        @pl.when(enc)
        def _():
            e_hop(i).wait_send()

        @pl.when(reg)
        def _():
            e_core(i).wait_send()
            d_hop(i).wait_send()


def fused(z, x, pg, wa, wu, wd, bias, norms, cols, keys):
    places, count = plan(z)
    I, R, D, BL, SL = z.images, z.rows, z.width, z.block, z.slots
    PW = z.pair
    KEYS = 2 * BL
    vm = pl.BlockSpec(memory_space=pltpu.VMEM)
    hbm = pl.BlockSpec(memory_space=pl.ANY)

    def b16(*shape):
        return pltpu.VMEM(shape, BF16)

    def f32(*shape):
        return pltpu.VMEM(shape, F32)

    scratch = [
        b16(3, D, D),
        b16(2, I, 2, SL, D),
        b16(I, SL, D),
        f32(8, D),
        b16(I, BL, D), b16(I, BL, D),
        b16(2, I, BL, D), b16(2, I, BL, D),
        b16(2, I, BL, PW), b16(2, I, BL, PW), b16(2, I, BL, PW), b16(2, I, BL, PW),
        b16(I, z.heads, KEYS, KEYS),
        f32(I, BL, D), f32(I, BL, D),
        b16(2, I, BL, D),
        b16(2, 2, R, D), b16(2, 2, R, D),
        f32(I, BL, D), f32(I, BL, D),
        b16(2, I, BL, D), b16(4, I, BL, D),
        b16(2, I, BL, D), b16(2, I, BL, D),
        b16(2, I, BL, PW), b16(2, I, BL, PW), b16(2, I, BL, PW), b16(2, I, BL, PW),
        b16(2, 3 * D, D),
        b16(3 * D, D), b16(3 * D, D), b16(3 * D, D),
        b16(2, I, BL, D),
        b16(2, I, 2, SL, D),
        f32(8, D), f32(5, 16, D), f32(16, D),
        pltpu.SemaphoreType.DMA((count,)),
        pltpu.SemaphoreType.DMA((count,)),
        pltpu.SemaphoreType.DMA((z.parts + 2,)),
    ]
    return pl.pallas_call(
        functools.partial(body, z, places),
        out_shape=(
            jax.ShapeDtypeStruct((2, I, SL, D), BF16),
            jax.ShapeDtypeStruct((2, I, SL, D), BF16),
            jax.ShapeDtypeStruct((3 * D, D), BF16),
            jax.ShapeDtypeStruct((16, D), F32),
        ),
        in_specs=[vm] * 9,
        out_specs=(hbm, hbm, hbm, vm),
        scratch_shapes=scratch,
        compiler_params=pltpu.CompilerParams(
            collective_id=0, has_side_effects=True, vmem_limit_bytes=121 * 2**19
        ),
    )(x, pg, wa, wu, wd, bias, norms, cols, keys)


def local(
    n_dp,
    block_in, lengths, patch_mask, pred_grad, w_qkv, w_out, w_up, w_down, qv_bias, mlp_bias, norms
):
    sec = lax.axis_index("section")
    t = lax.axis_index("tensor")
    y = t // 2
    images, slots, width = block_in.shape[1:]
    piece = w_qkv.shape[3]
    z = Sizes(n_dp, images // 2, slots, width, piece)

    x = block_in[0].reshape(2, z.images, slots, width)
    pg = pred_grad.reshape(2, z.images, slots, width)
    wa = jnp.concatenate([jnp.swapaxes(w_qkv[0], 1, 2).reshape(3 * piece, width), w_out[0]], axis=0)

    flat_q = jnp.zeros((1, width), F32)
    q_row, v_row = qv_bias[0, 0:1], qv_bias[0, 1:2]
    pad = jnp.zeros((1, width - piece), F32)
    pad2 = jnp.zeros((1, width - 2 * piece), F32)
    gap = jnp.zeros((1, piece), F32)
    bias = jnp.concatenate(
        [
            jnp.concatenate([q_row, pad], 1), jnp.concatenate([gap, q_row, pad2], 1),
            jnp.concatenate([v_row, pad], 1), jnp.concatenate([gap, v_row, pad2], 1),
            mlp_bias, flat_q, flat_q, flat_q,
        ],
        axis=0,
    )

    chip_lengths = lax.dynamic_slice_in_dim(lengths, y * z.images, z.images, 0)
    chip_mask = lax.dynamic_slice_in_dim(patch_mask, y * z.images, z.images, 0)
    order = [t, 2 * (1 - y) + t % 2, 2 * y + 1 - t % 2, 2 * (1 - y) + 1 - t % 2]
    positions = jnp.concatenate([j * slots + jnp.arange(slots, dtype=jnp.int32) for j in order])
    mask = jnp.concatenate(
        [lax.dynamic_slice_in_dim(chip_mask, j * slots, slots, 1) for j in order], axis=1
    )
    valid = positions[None, :] < chip_lengths[:, None]
    seen = (valid & (mask > 0)).astype(F32)
    covered = (valid & (mask == 0)).astype(F32)
    code = jnp.where(sec == 0, seen, 0.0)
    keys = jnp.where(valid, code, 2.0)[:, None, :]
    cols = jnp.stack([code, seen, covered, covered], axis=-1)
    cols = cols.reshape(z.images, 2, z.block, 4).swapaxes(0, 1)

    res, gin, grads, small = fused(
        z, x, pg, wa, w_up[0], w_down[0], bias, norms[0], cols, keys
    )
    g_down, g_up, g_attn = grads[:width], grads[width:2 * width], grads[2 * width:]
    g_qkv = jnp.swapaxes(g_attn[:3 * piece].reshape(3, piece, width), 1, 2).astype(F32)
    g_qv = small[10:12, :piece] + small[12:14, piece:2 * piece]
    return (
        res.reshape(1, images, slots, width),
        gin.reshape(1, images, slots, width).astype(F32),
        g_qkv[None],
        g_attn[3 * piece:].astype(F32)[None],
        g_up.astype(F32)[None],
        g_down.astype(F32)[None],
        g_qv[None],
        small[8:9],
        small[0:8][None],
    )


def solution(mesh):
    return jax.shard_map(
        functools.partial(local, mesh.shape["dp"]),
        mesh=mesh,
        in_specs=(
            P("section", "dp", "tensor", None),
            P("dp"),
            P("dp", None),
            P("dp", "tensor", None),
            P("section", None, None, "tensor"),
            P("section", "tensor", None),
            P("section", None, "tensor"),
            P("section", "tensor", None),
            P("section", None, "tensor"),
            P("section", "tensor"),
            P("section", None, None),
        ),
        out_specs=(
            P("section", "dp", "tensor", None),
            P("section", "dp", "tensor", None),
            P("section", None, None, "tensor"),
            P("section", "tensor", None),
            P("section", None, "tensor"),
            P("section", "tensor", None),
            P("section", None, "tensor"),
            P("section", "tensor"),
            P("section", None, None),
        ),
        check_vma=False,
    )
```

time: 1130 us -> 302 us (0.27); the launches traced: 1120 us -> 302 us
  waiting for transfers between devices: 580 us -> 0 us
  matrix products: 279 us -> 0 us
  Pallas kernels: 0 us -> 279 us
  other arithmetic: 109 us -> 12.8 us
  blocking collectives: 79.7 us -> 0 us
  local copies, waits for them, and re-layouts: 39.3 us -> 9.2 us
  between operations: 17.3 us -> 0.79 us
  starting transfers between devices: 12.2 us -> 0 us
    pallas_call x0 -> x1, Pallas kernels: none -> 279 us  [fused(): pl.pallas_call(functools.partial(body, z, places), out_shape=(jax.ShapeDt...]
    reduce_scatter x15 -> x0, waiting for transfers between devices: 276 us -> none  [the longest x3 77.5 us: forward_block(): lax.psum_scatter(rows_product(mixed_low, w_out).astype(jnp.bfloat16), 'te...]
    dot_general x69 -> x0, matrix products: 263 us -> none  [the longest x3 59.2 us: attn_back(): jnp.einsum('bhqk,bqhd->bkhd', d_raw, queries, preferred_element_type=jnp....]
    all_gather x14 -> x0, waiting for transfers between devices: 213 us -> none  [the longest x3 52.7 us: attn_back(): lax.all_gather(d_attended.astype(jnp.bfloat16), 'tensor', axis=1, tiled=T...]
    psum x2 -> x0, blocking collectives: 73.5 us -> none  [the longest x1 61.6 us: local(): norm_sum = lax.psum(norm_acc, ('dp', 'tensor'))]
    psum x1 -> x0, waiting for transfers between devices: 57.8 us -> none  [local(): lax.psum(attn_acc[0].astype(jnp.bfloat16), 'dp').astype(jnp.float32)]
    convert_element_type x21 -> x2, other arithmetic: 43.7 us -> 2.35 us  [the longest x1 2.17 us: local(): gin.reshape(1, images, slots, width).astype(F32)]
    reduce_sum x28 -> x0, other arithmetic: 37.9 us -> none  [the longest x13 23.5 us: layer_norm(): return centred * lax.rsqrt(spread + norm_epsilon) * norm_gain + norm_shift]
  transfers between devices with their start and end apart: 34 -> 0, of which waited for: 30 -> 0; matrix products, arithmetic and copies ran while one was open for 12% -> 0% of each run, Pallas kernels for 0% -> 0%
where the time goes in v1:
time: 302 us
  Pallas kernels  279 us (92%)
  other arithmetic  12.8 us (4%)
  local copies, waits for them, and re-layouts  9.2 us (3%)
    pallas_call x1, Pallas kernels, fused(): pl.pallas_call(functools.partial(body, z, places), out_shape=(jax.ShapeDt...  279 us

profile of v1, /device:TPU:0, one launch (start us, length us, event | category | flops | bytes accessed | tf_op | source)
XLA Modules:
  0.0 301.5 jit_solution(995943639301534337)
XLA Ops:
  0.7 0.8 dynamic_slice.16
  1.6 0.1 pad_add_fusion.1
  1.6 0.8 slice_bitcast_fusion.1
  2.4 0.1 maximum_maximum_fusion.1
  2.5 0.9 fusion.3
  3.4 0.7 compare_select_fusion.key_ref
  4.1 0.1 compare_bitcast_fusion.1
  4.2 1.3 concatenate.62.bias_ref
  5.5 0.2 copy.27
  5.8 0.2 copy.28
  6.0 0.1 broadcast_select_fusion
  6.2 0.2 fusion
  6.3 1.1 maximum_bitcast_fusion.col_ref
  7.5 1.1 pad_maximum_fusion.wa_ref
  8.6 278.8 %shard_map.178 = (bf16[2,3,64,768]{3,2,1,0:T(8,128)(2,1)}, bf16[2,3,64,768]{3,2,1,0:T(8,128)(2,1)}, bf16[2304,768]{1,0:T(8,128)(2,1)}, f32[16,768]{1,0:T(8,128)}) custom-call(bf16[2,3,64,768]{3,2,1,0:T(8,128)(2,1)} %bitcast.56, bf16[2,3,64,768]{3,2,1,0:T(8,128)(2,1)} %bitcast.57, bf16[768,768]{1,0:T(8,128)(2,1)} %pad_maximum_fusion.wa_ref, ...), custom_call_target="tpu_custom_call" | custom-call | tf_op jit(solution)/shard_map/pallas_call | solution.py:758
  287.3 1.4 add_bitcast_fusion
  288.8 1.3 slice.41
  290.1 1.3 slice_bitcast_fusion
  291.4 2.2 bitcast_convert_fusion.2
  293.6 1.8 bitcast_convert_fusion.3
  295.4 1.4 slice.35
  296.8 1.4 convert_bitcast_fusion
  298.2 2.5 bitcast_convert_fusion
  300.7 0.8 copy.30
  (19 shorter events, 0.1 us)
Async XLA Ops:
  0.7 6.8 %copy-start.1 = (bf16[1,3,768,192]{2,3,1,0:T(8,128)(2,1)S(1)}, bf16[1,3,768,192]{2,3,1,0:T(8,128)(2,1)}, u32[]{:S(2)}) copy-start(bf16[1,3,768,192]{2,3,1,0:T(8,128)(2,1)} %param.15) | copy-start | bytes 2654212
  0.7 6.8 %copy-start.3 = (bf16[1,192,768]{2,1,0:T(8,128)(2,1)S(1)}, bf16[1,192,768]{2,1,0:T(8,128)(2,1)}, u32[]{:S(2)}) copy-start(bf16[1,192,768]{2,1,0:T(8,128)(2,1)} %param.16) | copy-start | bytes 884740
  295.4 2.7 copy-start
  298.2 2.5 copy-start.2

commit v2 on v1

v2 whole, which is shorter than its diff:
```python
import functools

import jax
import jax.numpy as jnp
from jax import lax
from jax.experimental import pallas as pl
from jax.experimental.pallas import tpu as pltpu
from jax.sharding import PartitionSpec as P

HD = 64
CH = 128
GC = 64
AROUND = (2, 1, 1)
EPS = 1e-06
MASKED = -1000000000.0
F32 = jnp.float32
BF16 = jnp.bfloat16


class Places:
    def __init__(self):
        self.count = 0

    def take(self, many=1):
        first = self.count
        self.count += many
        return first


def nn(a, b):
    return lax.dot_general(a, b, (((1,), (0,)), ((), ())), preferred_element_type=F32)


def nt(a, b):
    return lax.dot_general(a, b, (((1,), (1,)), ((), ())), preferred_element_type=F32)


def tn(a, b):
    return lax.dot_general(a, b, (((0,), (0,)), ((), ())), preferred_element_type=F32)


def normal(u):
    mean = jnp.mean(u, axis=-1, keepdims=True)
    centred = u - mean
    spread = jnp.mean(centred * centred, axis=-1, keepdims=True)
    inverse = lax.rsqrt(spread + EPS)
    return centred * inverse, inverse


def normal_back(hat, inverse, grad):
    first = jnp.mean(grad, axis=-1, keepdims=True)
    second = jnp.mean(grad * hat, axis=-1, keepdims=True)
    return inverse * (grad - first - hat * second)


def column_sum(u):
    return jnp.sum(u, axis=0, keepdims=True)


class Sizes:
    def __init__(self, n_dp, images, slots, width, piece):
        self.n_dp = n_dp
        self.images = images
        self.slots = slots
        self.width = width
        self.piece = piece
        self.block = 2 * slots
        self.rows = images * self.block
        self.pair = 2 * piece
        self.heads = self.pair // HD
        self.around = sum(AROUND)
        self.per_mat = width // GC
        self.parts = 3 * self.per_mat


def plan(z):
    p, d, n = Places(), Places(), Places()
    pieces = z.width // CH
    recv = dict(
        x=p.take(), bias=p.take(2), xc0=p.take(), xc1=p.take(), pg=p.take(),
        wy=p.take(3 * pieces), wz=p.take(3 * pieces // 2),
        d1=p.take(z.around), d2=p.take(z.around),
        e=p.take(z.images), ec=p.take(z.images),
        attn=p.take(z.images), h2=p.take(z.images), br=p.take(z.images), dbl=p.take(z.images),
        dh2=p.take(), dal=p.take(), dn=p.take(z.images),
        dlat=p.take(z.images), res=p.take(), gin=p.take(),
        gy=p.take(z.parts), ga=p.take(z.parts), gb=p.take(z.parts),
        sy=p.take(), sc=p.take(), sa=p.take(), sb=p.take(),
    )
    together = ("wy", "wz", "d1", "gy", "ga", "gb", "attn", "h2", "br", "dbl", "e", "ec", "dlat", "dn")
    many = dict(bias=2, d2=z.around)
    send = {name: d.take(many.get(name, 1)) for name in recv}
    send["d3"] = d.take(z.around)
    local = {name: n.take() for name in ("w0", "w1", "w2", "x", "pg", "res", "gin", "g0", "g1", "g2")}
    return recv, send, frozenset(together), local, p.count, d.count, n.count


def body(
    z, places,
    x_ref, pg_ref, wa_ref, wu_ref, wd_ref, len_ref, mask_ref, qv_ref, mlp_ref, norm_ref,
    res_ref, gin_ref, gd_ref, gu_ref, ga_ref, small_ref,
    wown, wy, xall, pgr, qv_y, mlp_y, code_c, seen_c, cov_c, key_r,
    e_own, e_oth, h, kv, q, kk, vv, o, p, att, mid, h2, act, gp, brv, dy,
    snd, rcv, dbl, dal, dol, dq, dk, dv, g, yr, za, zb, dlat, outb, nacc, sml, small_in,
    ss, rs, ls,
):
    S, SEND, TOGETHER, LOCAL = places
    sec = lax.axis_index("section")
    dp = lax.axis_index("dp")
    t = lax.axis_index("tensor")
    y = t // 2
    c = t % 2
    to_y = {"tensor": 2 * (1 - y) + c}
    to_c = {"tensor": 2 * y + 1 - c}
    to_s = {"section": 1 - sec}
    parity = dp % 2
    pair_z = {"dp": dp + 1 - 2 * parity}
    top = dp // (z.n_dp // 2)
    to_m = {"dp": dp + 1 - 2 * top}
    to_w = {"dp": dp - 1 + 2 * top}
    is_end = jnp.logical_or(dp == 0, dp == z.n_dp - 1)
    not_end = jnp.logical_not(is_end)
    is_mid = jnp.logical_or(dp == z.n_dp // 2 - 1, dp == z.n_dp // 2)
    not_mid = jnp.logical_not(is_mid)
    enc = sec == 0
    reg = sec == 1

    I, R, D, BL, SL = z.images, z.rows, z.width, z.block, z.slots
    PC, PW = z.piece, z.pair
    KEYS = 2 * BL
    WP = D // CH
    HELP = (2, WP // 2)

    def far(src, dst, name, to, index=0, receive=None, send=None):
        leave = SEND[send or name] + (0 if name in TOGETHER else index)
        return pltpu.make_async_remote_copy(
            src_ref=src, dst_ref=dst, send_sem=ss.at[leave], recv_sem=rs.at[S[receive or name] + index],
            device_id=to, device_id_type=pl.DeviceIdType.MESH,
        )

    def gone(ref, name, to):
        far(ref, ref, name, to).wait_send()

    def here(src, dst, name):
        return pltpu.make_async_copy(src, dst, ls.at[LOCAL[name]])

    w_refs = (wa_ref, wu_ref, wd_ref)
    own_w = [here(w_refs[m], wown.at[m], ("w0", "w1", "w2")[m]) for m in range(3)]
    own_x = here(x_ref.at[y], xall.at[0, :, 0], "x")
    own_pg = here(pg_ref.at[y], pgr.at[0], "pg")
    own_x.start()
    for copy in own_w:
        copy.start()
    own_pg.start()

    barrier = pltpu.get_barrier_semaphore()

    def greet(to):
        pl.semaphore_signal(barrier, inc=1, device_id=to, device_id_type=pl.DeviceIdType.MESH)

    greet(to_y)
    greet(to_c)
    greet(to_s)
    greet(to_m)

    @pl.when(not_end)
    def _():
        greet(to_w)
        pl.semaphore_wait(barrier, 5)

    @pl.when(is_end)
    def _():
        pl.semaphore_wait(barrier, 4)

    c_x = far(x_ref.at[1 - y], xall.at[0, :, 1], "x", to_y)
    c_b0 = far(qv_ref, qv_y, "bias", to_y)
    c_b1 = far(mlp_ref, mlp_y, "bias", to_y, 1)
    c_xc0 = far(x_ref.at[y], xall.at[1, :, 0], "xc0", to_c)
    c_xc1 = far(xall.at[0, :, 1], xall.at[1, :, 1], "xc1", to_c)
    c_pg = far(pg_ref.at[1 - y], pgr.at[1], "pg", to_y)

    def rows_of(j, side):
        return pl.ds(pl.multiple_of((j + side * (WP - 1 - 2 * j)) * CH, CH), CH)

    def w_y(m, j):
        at = rows_of(j, parity)
        return far(w_refs[m].at[at], wy.at[m, at], "wy", to_y, m * WP + j)

    def w_z(m, j, side=None):
        at = rows_of(j, parity if side is None else side)
        return far(wy.at[m, at], wy.at[m, at], "wz", pair_z, m * (WP // 2) + j)

    around = [(m, WP - HELP[0] - 1 - j) for m in range(3) for j in range(AROUND[m] - 1, -1, -1)]

    def d_slot(side, n):
        return g.at[side, pl.ds(n * CH, CH)]

    def d_out(n):
        m, j = around[n]
        return far(w_refs[m].at[rows_of(j, parity)], d_slot(0, n), "d1", to_s, n)

    def d_over(n):
        return far(d_slot(0, n), d_slot(1, n), "d2", to_y, n)

    def d_back(n):
        m, j = around[n]
        leave = SEND["d3"] + n
        return pltpu.make_async_remote_copy(
            src_ref=d_slot(1, n), dst_ref=wy.at[m, rows_of(j, parity)],
            send_sem=ss.at[leave], recv_sem=rs.at[S["wy"] + m * WP + j],
            device_id=to_s, device_id_type=pl.DeviceIdType.MESH,
        )

    straight = (
        [[j for j in range(WP - HELP[0]) if (m, j) not in around] for m in range(3)],
        [list(range(WP - HELP[1])) for m in range(3)],
    )

    def start_inputs():
        c_x.start()
        c_b0.start()
        c_b1.start()
        c_xc0.start()

    @pl.when(enc)
    def _():
        for n in range(len(around)):
            d_out(n).start()
        start_inputs()
        for m in range(3):
            for j in straight[0][m]:
                w_y(m, j).start()

    @pl.when(reg)
    def _():
        for n in range(len(around) + 1):
            if n < len(around):
                d_out(n).wait_recv()
                d_over(n).start()
            if n > 0:
                d_over(n - 1).wait_recv()
                d_back(n - 1).start()
            if n == max(len(around) - 1, 0):
                start_inputs()
                for m in range(3):
                    for j in straight[1][m]:
                        w_y(m, j).start()
                c_pg.start()
        for n in range(len(around)):
            d_over(n).wait_send()
            d_back(n).wait_send()

    def forward_w(m, j):
        for s, flag in enumerate((enc, reg)):
            @pl.when(jnp.logical_and(flag, j < HELP[s]))
            def _():
                w_y(m, j).wait_recv()
                w_z(m, j).start()

    def finish_w(m):
        for s, flag in enumerate((enc, reg)):
            @pl.when(flag)
            def _():
                for j in range(HELP[s], WP - HELP[s]):
                    w_y(m, j).wait_recv()
                for j in range(HELP[s]):
                    w_z(m, j, 1 - parity).wait_recv()

    rank = lax.broadcasted_iota(jnp.int32, (KEYS, KEYS), 0)
    across = lax.broadcasted_iota(jnp.int32, (KEYS, KEYS), 1)
    group = rank // SL
    y_of = y + (group % 2) * (1 - 2 * y)
    c_of = c + (group // 2) * (1 - 2 * c)
    slot = (2 * y_of + c_of) * SL + rank % SL
    here_slot = slot == across
    diagonal = rank == across
    slot_col = slot[:, 0:1]
    for i in range(I):
        picked = jnp.where(here_slot, mask_ref[pl.ds(y * I + i, 1), :].astype(F32), 0.0)
        marked = jnp.sum(picked, axis=1, keepdims=True) > 0.5
        valid = slot_col < len_ref[y * I + i]
        seen = jnp.where(jnp.logical_and(valid, marked), 1.0, 0.0)
        code = jnp.where(enc, seen, jnp.zeros_like(seen))
        seen_c[i] = seen
        cov_c[i] = jnp.where(valid, 1.0, 0.0) - seen
        code_c[i] = code
        key = jnp.where(valid, code, 2.0)
        key_r[i] = jnp.sum(jnp.where(diagonal, key, 0.0), axis=0, keepdims=True)

    g0, b0 = norm_ref[0:1, :], norm_ref[1:2, :]

    def lay(block):
        return block.reshape(BL, D)

    own_x.wait()
    c_x.wait_recv()
    c_xc1.start()

    def norm_rows(half):
        def one(i, carry):
            hat, _ = normal(lay(xall[half, i]).astype(F32))
            value = (hat * g0 + b0).astype(BF16)
            h[half, i] = value
            kv[half, i] = value
            return carry

        lax.fori_loop(0, I, one, 0)

    norm_rows(0)
    c_xc0.wait_recv()
    c_xc1.wait_recv()
    norm_rows(1)
    for j in range(HELP[1]):
        forward_w(0, j)
    c_b0.wait_recv()
    c_b1.wait_recv()
    own_w[0].wait()
    finish_w(0)

    def both_rows(first, many):
        return jnp.concatenate([wown[0, first:first + many], wy[0, first:first + many]], axis=0)

    bq = jnp.concatenate([qv_ref[0:1, :], qv_y[0:1, :]], axis=1)
    bv = jnp.concatenate([qv_ref[1:2, :], qv_y[1:2, :]], axis=1)

    def flat(ref, half):
        return ref[half].reshape(R, ref.shape[-1])

    def e_hop(i):
        return far(dlat.at[0, i], e_own.at[i], "e", to_s, i)

    def e_core(i):
        return far(e_own.at[i], e_oth.at[i], "ec", to_c, i)

    for half in range(2):
        q[half] = ((nt(flat(h, half), both_rows(0, PC)) + bq).astype(BF16) * 0.125).reshape(I, BL, PW)

    lane = lax.broadcasted_iota(jnp.int32, (KEYS, 2 * HD), 1)
    lanes = (lane < HD, lane >= HD)
    zero16 = jnp.zeros((KEYS, 2 * HD), BF16)

    def image(ref, i, pr):
        at = slice(pr * 2 * HD, (pr + 1) * 2 * HD)
        return jnp.concatenate([ref[0, i, :, at], ref[1, i, :, at]], axis=0)

    def put(ref, i, pr, value):
        at = slice(pr * 2 * HD, (pr + 1) * 2 * HD)
        ref[0, i, :, at] = value[:BL]
        ref[1, i, :, at] = value[BL:]

    def latent_keys(half, ref, i):
        hat, _ = normal(ref[i].astype(F32))
        value = (hat * g0 + b0).astype(BF16)
        seen = seen_c[i, half * BL:(half + 1) * BL] > 0.5
        kv[half, i] = jnp.where(seen, value, h[half, i])

    def attend(i):
        @pl.when(reg)
        def _():
            e_hop(i).wait_recv()
            e_core(i).start()
            latent_keys(0, e_own, i)
            e_core(i).wait_recv()
            latent_keys(1, e_oth, i)

        rows_k = kv[:, i].reshape(KEYS, D)
        kk[:, i] = nt(rows_k, both_rows(PC, PC)).astype(BF16).reshape(2, BL, PW)
        vv[:, i] = (nt(rows_k, both_rows(2 * PC, PC)) + bv).astype(BF16).reshape(2, BL, PW)
        shut = jnp.where(code_c[i] == key_r[i], 0.0, MASKED)
        for pr in range(z.heads // 2):
            qp, kp, vp = image(q, i, pr), image(kk, i, pr), image(vv, i, pr)
            outs = []
            for sub in range(2):
                scores = nt(jnp.where(lanes[sub], qp, zero16), kp) + shut
                top_value = jnp.max(scores, axis=-1, keepdims=True)
                e = jnp.exp(scores - top_value)
                probs = (e * (1.0 / jnp.sum(e, axis=-1, keepdims=True))).astype(BF16)
                p[i, 2 * pr + sub] = probs
                outs.append(nn(probs, vp))
            put(o, i, pr, jnp.where(lanes[0], outs[0], outs[1]).astype(BF16))
        attn = nn(o[:, i].reshape(KEYS, PW), both_rows(3 * PC, PC))
        snd[0, i] = attn[BL:].astype(BF16)
        exchange(0, "attn", i).start()
        att[i] = attn[:BL]

    def exchange(slot, name, i):
        return far(snd.at[slot % 2, i], rcv.at[slot, i], name, to_c, i)

    def h2_core(i):
        return far(h2.at[0, i], h2.at[1, i], "h2", to_c, i)

    def middle(i):
        exchange(0, "attn", i).wait_recv()
        attn = att[i] + rcv[0, i].astype(F32) + norm_ref[2:3, :]
        att[i] = attn
        value = lay(xall[0, i]).astype(F32) + norm_ref[3:4, :] * attn
        mid[i] = value
        hat, _ = normal(value)
        h2[0, i] = (hat * norm_ref[4:5, :] + norm_ref[5:6, :]).astype(BF16)
        h2_core(i).start()

    TW = 256
    NT = D // TW

    def rows_at(i):
        return pl.ds(i * BL, BL)

    def up(i, w, w_ref, b_row):
        rows2 = h2[:, i].reshape(KEYS, D)

        def one(n, carry):
            at = pl.ds(pl.multiple_of(n * TW, TW), TW)
            u = nn(rows2, w_ref[:, at]) + b_row[:, at]
            cdf = 0.5 + 0.5 * lax.erf(u * 0.7071067811865476)
            act[w, :, rows_at(i), at] = (u * cdf).astype(BF16).reshape(2, BL, TW)
            slope = cdf + u * (0.3989422804014327 * jnp.exp(-0.5 * u * u))
            gp[w, :, rows_at(i), at] = slope.astype(BF16).reshape(2, BL, TW)
            return carry

        lax.fori_loop(0, NT, one, 0)

    def down(i):
        br = nn(act[0, :, rows_at(i)].reshape(KEYS, D), wown[2])
        br += nn(act[1, :, rows_at(i)].reshape(KEYS, D), wy[2])
        snd[1, i] = br[BL:].astype(BF16)
        exchange(1, "br", i).start()
        brv[i] = br[:BL]

    def finish(i):
        exchange(1, "br", i).wait_recv()
        br = brv[i] + rcv[1, i].astype(F32) + norm_ref[6:7, :]
        brv[i] = br
        out = mid[i] + norm_ref[7:8, :] * br

        @pl.when(enc)
        def _():
            dlat[0, i] = (out * seen_c[i, :BL]).astype(BF16)
            e_hop(i).start()

        outb[0, i] = (out * cov_c[i, :BL]).astype(BF16).reshape(2, SL, D)

    def own_up(i):
        h2_core(i).wait_recv()
        up(i, 0, wown.at[1], mlp_ref)

    def other_up(i):
        up(i, 1, wy.at[1], mlp_y)

    for i in range(I + 2):
        if i < I:
            attend(i)
            if i < 2:
                for j in range(i * HELP[1] // 2, (i + 1) * HELP[1] // 2):
                    forward_w(1, j)
            middle(i)
        if i == 1:
            own_w[1].wait()
        if 1 <= i <= I:
            own_up(i - 1)
            for j in range((i - 1) * HELP[1] // I, i * HELP[1] // I):
                forward_w(2, j)
            if i == 1:
                finish_w(1)
            other_up(i - 1)
        if i == I:
            own_w[2].wait()
            finish_w(2)
            for n in range(I - 1):
                down(n)
        if i == I + 1:
            down(I - 1)
            for n in range(I):
                finish(n)
    w_o = both_rows(3 * PC, PC)

    def deliver(which, number, ref):
        return (
            here(outb.at[which, :, 0], ref.at[y], number),
            far(outb.at[which, :, 1], ref.at[y], number, to_y),
        )

    for copy in deliver(0, "res", res_ref):
        copy.start()

    nacc[...] = jnp.zeros_like(nacc)
    small_in[...] = jnp.zeros_like(small_in)

    def add_norm(row, value):
        nacc[row:row + 1, :] += value

    def d_hop(i):
        return far(dlat.at[0, i], dlat.at[1, i], "dlat", to_s, i)

    def dbl_core(i):
        return far(dbl.at[0, i], dbl.at[1, i], "dbl", to_c, i)

    own_pg.wait()

    @pl.when(reg)
    def _():
        c_pg.wait_recv()

    def start_back(i, carry):
        @pl.when(reg)
        def _():
            dy[i] = jnp.concatenate([pgr[0, i], pgr[1, i]], axis=0).astype(F32) * cov_c[i, :BL]

        @pl.when(enc)
        def _():
            d_hop(i).wait_recv()
            dy[i] = dlat[1, i].astype(F32) * seen_c[i, :BL]

        grad = dy[i]
        d_branch = norm_ref[7:8, :] * grad
        dbl[0, i] = d_branch.astype(BF16)
        dbl_core(i).start()
        add_norm(7, column_sum(grad * brv[i]))
        add_norm(6, column_sum(d_branch))
        return carry

    lax.fori_loop(0, I, start_back, 0)
    for i in range(I):
        dbl_core(i).wait_recv()

    N = z.parts
    PM = z.per_mat

    def part(k):
        return pl.ds(pl.multiple_of(k * GC, GC), GC)

    def y_part(k):
        at = part(k)
        return far(g.at[1, at], yr.at[at], "gy", to_y, k)

    def to_middle(k):
        at = part(k)

        @pl.when(is_mid)
        def _():
            far(g.at[0, at], zb.at[at], "ga", to_m, k, receive="gb").start()

        @pl.when(not_mid)
        def _():
            far(g.at[0, at], za.at[at], "ga", to_m, k).start()

    def from_away(k):
        at = part(k)
        return far(g.at[0, at], za.at[at], "ga", to_w, k)

    def total(k):
        at = part(k)
        return far(zb.at[at], zb.at[at], "gb", to_w, k)

    def stage0(k):
        at = part(k)
        y_part(k).wait_recv()
        g[0, at, :] = (g[0, at, :].astype(F32) + yr[at, :].astype(F32)).astype(BF16)

        @pl.when(is_end)
        def _():
            to_middle(k)

    def stage1(k):
        at = part(k)

        @pl.when(not_end)
        def _():
            from_away(k).wait_recv()
            g[0, at, :] = (g[0, at, :].astype(F32) + za[at, :].astype(F32)).astype(BF16)
            to_middle(k)

    def each_out(k, do):
        for m, ref in enumerate((gd_ref, gu_ref, ga_ref)):
            @pl.when(jnp.logical_and(k >= m * PM, k < (m + 1) * PM))
            def _():
                do(here(zb.at[part(k)], ref.at[part(k - m * PM)], ("g0", "g1", "g2")[m]))

    def stage2(k):
        at = part(k)
        total(k).wait_recv()

        @pl.when(is_mid)
        def _():
            zb[at, :] = (g[0, at, :].astype(F32) + zb[at, :].astype(F32)).astype(BF16)

        @pl.when(not_end)
        def _():
            total(k).start()

        each_out(k, lambda copy: copy.start())

    AWAY_LAG = 2
    MID_LAG = 4
    LAG = 8

    def small_middle(start):
        @pl.when(is_mid)
        def _():
            copy = far(sml.at[1], sml.at[4], "sa", to_m, receive="sb")
            copy.start() if start else copy.wait_send()

        @pl.when(not_mid)
        def _():
            copy = far(sml.at[1], sml.at[3], "sa", to_m)
            copy.start() if start else copy.wait_send()

    c_sy = far(small_in, sml.at[0], "sy", to_y)
    c_sc = far(sml.at[1], sml.at[2], "sc", to_c)
    s_total = far(sml.at[4], sml.at[4], "sb", to_w)

    def small0():
        c_sy.wait_recv()
        sml[1, 0:8, :] = small_in[0:8, :] + sml[0, 0:8, :]
        sml[1, 8:9, :] = small_in[8:9, :] + sml[0, 9:10, :]
        sml[1, 9:10, :] = jnp.zeros((1, D), F32)
        sml[1, 10:12, :] = small_in[10:12, :]
        sml[1, 12:14, :] = sml[0, 10:12, :]
        sml[1, 14:16, :] = jnp.zeros((2, D), F32)
        c_sc.start()

    def small1():
        c_sc.wait()
        sml[1, 0:8, :] = sml[1, 0:8, :] + sml[2, 0:8, :]

        @pl.when(is_end)
        def _():
            small_middle(True)

    def small2():
        @pl.when(not_end)
        def _():
            far(sml.at[1], sml.at[3], "sa", to_w).wait_recv()
            sml[1] = sml[1] + sml[3]
            small_middle(True)

    def small3():
        s_total.wait_recv()

        @pl.when(is_mid)
        def _():
            sml[4] = sml[1] + sml[4]

        @pl.when(not_end)
        def _():
            s_total.start()

        small_ref[...] = sml[4]

    def step(k, carry=0):
        @pl.when(k < N)
        def _():
            stage0(k)

        @pl.when(jnp.logical_and(k >= AWAY_LAG, k < N + AWAY_LAG))
        def _():
            stage1(k - AWAY_LAG)

        @pl.when(jnp.logical_and(is_mid, jnp.logical_and(k >= MID_LAG, k < N + MID_LAG)))
        def _():
            stage2(k - MID_LAG)

        @pl.when(jnp.logical_and(not_mid, jnp.logical_and(k >= LAG, k < N + LAG)))
        def _():
            stage2(k - LAG)

        pl.when(k == N - 6)(small0)
        pl.when(k == N - 5)(small1)
        pl.when(k == N - 4)(small2)
        pl.when(jnp.logical_and(is_mid, k == N - 2))(small3)
        pl.when(jnp.logical_and(not_mid, k == N))(small3)
        return carry

    done_steps = [0]

    def pump(many, index=0, times=1):
        first = done_steps[0] + index * many
        done_steps[0] += many * times

        @pl.when(enc)
        def _():
            lax.fori_loop(first, first + many, step, 0)

    first_down, first_up, first_attn = 0, PM, 2 * PM
    PT = TW // GC

    def outer_rows(left, right, w, first):
        def one(n, carry):
            at = pl.ds(pl.multiple_of(n * TW, TW), TW)
            to = pl.ds(pl.multiple_of(first * GC + n * TW, TW), TW)
            g[w, to, :] = tn(left(at), right()).astype(BF16)
            if w == 1:
                for k in range(PT):
                    y_part(first + n * PT + k).start()
            return carry

        lax.fori_loop(0, NT, one, 0)

    def wide(ref, w):
        return lambda at: ref[w, :, :, at].reshape(2 * R, at.size)

    def h2_cols(at):
        return jnp.concatenate(
            [h2[0, :, :, at].reshape(R, at.size), h2[1, :, :, at].reshape(R, at.size)], axis=0
        )

    def down_outer(w):
        outer_rows(wide(act, w), lambda: dbl[...].reshape(2 * R, D), w, first_down)

    def up_outer(w):
        outer_rows(h2_cols, lambda: gp[w].reshape(2 * R, D), w, first_up)

    @pl.when(enc)
    def _():
        down_outer(1)
        down_outer(0)

    def down_back(half, w, w_ref):
        rows = flat(dbl, half)

        def one(n, carry):
            at = pl.ds(pl.multiple_of(n * TW, TW), TW)
            du = nt(rows, w_ref[at, :]) * gp[w, half, :, at].astype(F32)
            small_in[8 + w:9 + w, at] += column_sum(du)
            gp[w, half, :, at] = du.astype(BF16)
            return carry

        lax.fori_loop(0, NT, one, 0)

    down_back(1, 1, wy.at[2])
    pump(1)
    down_back(1, 0, wown.at[2])
    pump(1)

    def up_back(half):
        return nt(gp[0, half], wown[1]) + nt(gp[1, half], wy[1])

    gone(snd.at[0], "attn", to_c)
    snd[0] = up_back(1).astype(BF16).reshape(I, BL, D)
    c_dh2 = far(snd.at[0], rcv.at[2], "dh2", to_c)
    c_dh2.start()
    pump(1)
    down_back(0, 1, wy.at[2])
    pump(1)
    down_back(0, 0, wown.at[2])

    @pl.when(enc)
    def _():
        up_outer(1)

    pump(1)

    @pl.when(enc)
    def _():
        up_outer(0)

    pump(1)
    back0 = up_back(0).reshape(I, BL, D)
    c_dh2.wait_recv()

    for i in range(I):
        grad = back0[i] + rcv[2, i].astype(F32)
        hat, inverse = normal(mid[i])
        add_norm(4, column_sum(grad * hat))
        add_norm(5, column_sum(grad))
        d_mid = dy[i] + normal_back(hat, inverse, grad * norm_ref[4:5, :])
        dy[i] = d_mid
        add_norm(3, column_sum(d_mid * att[i]))
        d_att = norm_ref[3:4, :] * d_mid
        add_norm(2, column_sum(d_att))
        dal[0, i] = d_att.astype(BF16)
    c_dal = far(dal.at[0], dal.at[1], "dal", to_c)
    c_dal.start()
    pump(1)

    dol[0] = nt(flat(dal, 0), w_o).astype(BF16).reshape(I, BL, PW)
    c_dal.wait_recv()
    dol[1] = nt(flat(dal, 1), w_o).astype(BF16).reshape(I, BL, PW)
    pump(1)

    def all_rows(ref):
        return ref[...].reshape(2 * R, ref.shape[-1])

    base = first_attn * GC

    def store_rows(value, first):
        g[0, base + first:base + first + PC, :] = value[:PC].astype(BF16)
        g[1, base + first:base + first + PC, :] = value[PC:].astype(BF16)

    def attend_back(i):
        for pr in range(z.heads // 2):
            qp, kp, vp, gpair = image(q, i, pr), image(kk, i, pr), image(vv, i, pr), image(dol, i, pr)
            at = slice(pr * 2 * HD, (pr + 1) * 2 * HD)
            dqs, dks, dvs = [], [], []
            for sub in range(2):
                probs = p[i, 2 * pr + sub]
                wide_probs = probs.astype(F32)
                d_probs = nt(jnp.where(lanes[sub], gpair, zero16), vp)
                dvs.append(tn(probs, gpair))
                inner = jnp.sum(d_probs * wide_probs, axis=-1, keepdims=True)
                ds = (wide_probs * (d_probs - inner)).astype(BF16)
                dqs.append(nn(ds, kp))
                dks.append(tn(ds, qp))
            d_q = jnp.where(lanes[0], dqs[0], dqs[1]) * 0.125
            d_k = jnp.where(lanes[0], dks[0], dks[1])
            d_v = jnp.where(lanes[0], dvs[0], dvs[1])
            small_in[10:11, at] += column_sum(d_q)
            small_in[11:12, at] += column_sum(d_v)
            put(dq, i, pr, d_q.astype(BF16))
            put(dk, i, pr, d_k.astype(BF16))
            put(dv, i, pr, d_v.astype(BF16))

    def dn_core(i):
        return far(snd.at[1, i], rcv.at[3, i], "dn", to_c, i)

    def input_back(i):
        grad = nn(dq[:, i].reshape(KEYS, PW), both_rows(0, PC))
        grad += nn(dk[:, i].reshape(KEYS, PW), both_rows(PC, PC))
        grad += nn(dv[:, i].reshape(KEYS, PW), both_rows(2 * PC, PC))
        snd[1, i] = grad[BL:].astype(BF16)
        dn_core(i).start()
        back1[i] = grad[:BL]

    def leave(i):
        dn_core(i).wait_recv()
        grad = back1[i] + rcv[3, i].astype(F32)
        extra = jnp.logical_and(seen_c[i, :BL] > 0.5, reg)

        @pl.when(reg)
        def _():
            other = jnp.where(extra, grad, 0.0)
            hat, inverse = normal(e_own[i].astype(F32))
            dlat[0, i] = normal_back(hat, inverse, other * g0).astype(BF16)
            d_hop(i).start()
            add_norm(0, column_sum(other * hat))
            add_norm(1, column_sum(other))

        own = jnp.where(extra, 0.0, grad)
        hat, inverse = normal(lay(xall[0, i]).astype(F32))
        add_norm(0, column_sum(own * hat))
        add_norm(1, column_sum(own))
        d_x = dy[i] + normal_back(hat, inverse, own * g0)
        outb[1, i] = d_x.astype(BF16).reshape(2, SL, D)

    back1 = brv
    gone(snd.at[1], "br", to_c)
    for i in range(I):
        attend_back(i)
        pump(1)
        input_back(i)
        pump(1)
        if i > 0:
            leave(i - 1)
    leave(I - 1)
    pump(1)

    @pl.when(reg)
    def _():
        down_outer(1)
        down_outer(0)
        up_outer(1)
        up_outer(0)

    store_rows(tn(all_rows(dq), all_rows(h)), 0)
    pump(1)
    store_rows(tn(all_rows(dk), all_rows(kv)), PC)
    pump(1)
    store_rows(tn(all_rows(dv), all_rows(kv)), 2 * PC)
    pump(1)
    store_rows(tn(all_rows(o), all_rows(dal)), 3 * PC)
    small_in[0:8, :] = nacc[...]
    c_sy.start()
    for k in range(first_attn, z.parts):
        y_part(k).start()
    for copy in deliver(1, "gin", gin_ref):
        copy.start()

    lax.fori_loop(jnp.where(enc, done_steps[0], 0), N + LAG, step, 0)

    small_middle(False)
    gone(g.at[1], "gy", to_y)
    gone(g.at[0], "ga", to_m)

    @pl.when(not_end)
    def _():
        s_total.wait_send()
        gone(zb, "gb", to_w)

    c_sy.wait_send()
    for m, ref in enumerate((gd_ref, gu_ref, ga_ref)):
        here(zb.at[0:D], ref, ("g0", "g1", "g2")[m]).wait()
    for which, number, ref in ((0, "res", res_ref), (1, "gin", gin_ref)):
        for copy in deliver(which, number, ref):
            copy.wait()
    for copy in (c_x, c_b0, c_b1, c_xc0, c_xc1, c_dh2, c_dal):
        copy.wait_send()
    gone(h2.at[0], "h2", to_c)
    gone(dbl.at[0], "dbl", to_c)
    gone(snd.at[1], "dn", to_c)

    @pl.when(enc)
    def _():
        if around:
            gone(g.at[0, 0:len(around) * CH], "d1", to_s)
        gone(e_own, "e", to_s)

    @pl.when(reg)
    def _():
        c_pg.wait_send()
        gone(e_own, "ec", to_c)
        gone(dlat.at[0], "dlat", to_s)

    for s, flag in enumerate((enc, reg)):
        @pl.when(flag)
        def _():
            gone(g.at[0, 0:sum(len(js) for js in straight[s]) * CH], "wy", to_y)
            gone(g.at[0, 0:3 * HELP[s] * CH], "wz", pair_z)


def fused(z, x, pg, wa, wu, wd, lengths, mask, qv, mlp, norms):
    *places, arrivals, departures, copies = plan(z)
    I, R, D, BL, SL = z.images, z.rows, z.width, z.block, z.slots
    PC, PW = z.piece, z.pair
    KEYS = 2 * BL
    vm = pl.BlockSpec(memory_space=pltpu.VMEM)
    sm = pl.BlockSpec(memory_space=pltpu.SMEM)
    hbm = pl.BlockSpec(memory_space=pl.ANY)

    def b16(*shape):
        return pltpu.VMEM(shape, BF16)

    def f32(*shape):
        return pltpu.VMEM(shape, F32)

    scratch = [
        b16(3, D, D), b16(3, D, D),
        b16(2, I, 2, SL, D),
        b16(2, I, SL, D),
        f32(2, PC), f32(1, D),
        f32(I, KEYS, 1), f32(I, KEYS, 1), f32(I, KEYS, 1), f32(I, 1, KEYS),
        b16(I, BL, D), b16(I, BL, D),
        b16(2, I, BL, D), b16(2, I, BL, D),
        b16(2, I, BL, PW), b16(2, I, BL, PW), b16(2, I, BL, PW), b16(2, I, BL, PW),
        b16(I, z.heads, KEYS, KEYS),
        f32(I, BL, D), f32(I, BL, D),
        b16(2, I, BL, D),
        b16(2, 2, R, D), b16(2, 2, R, D),
        f32(I, BL, D), f32(I, BL, D),
        b16(2, I, BL, D), b16(4, I, BL, D),
        b16(2, I, BL, D), b16(2, I, BL, D),
        b16(2, I, BL, PW), b16(2, I, BL, PW), b16(2, I, BL, PW), b16(2, I, BL, PW),
        b16(2, 3 * D, D),
        b16(3 * D, D), b16(3 * D, D), b16(3 * D, D),
        b16(2, I, BL, D),
        b16(2, I, 2, SL, D),
        f32(8, D), f32(5, 16, D), f32(16, D),
        pltpu.SemaphoreType.DMA((departures,)),
        pltpu.SemaphoreType.DMA((arrivals,)),
        pltpu.SemaphoreType.DMA((copies,)),
    ]
    weight = jax.ShapeDtypeStruct((D, D), BF16)
    rows = jax.ShapeDtypeStruct((2, I, SL, D), BF16)
    return pl.pallas_call(
        functools.partial(body, z, places),
        out_shape=(rows, rows, weight, weight, weight, jax.ShapeDtypeStruct((16, D), F32)),
        in_specs=[hbm] * 5 + [sm] + [vm] * 4,
        out_specs=(hbm, hbm, hbm, hbm, hbm, vm),
        scratch_shapes=scratch,
        compiler_params=pltpu.CompilerParams(
            collective_id=0, has_side_effects=True, vmem_limit_bytes=121 * 2**19
        ),
    )(x, pg, wa, wu, wd, lengths, mask, qv, mlp, norms)


def local(
    n_dp,
    block_in, lengths, patch_mask, pred_grad, w_qkv, w_out, w_up, w_down, qv_bias, mlp_bias, norms
):
    images, slots, width = block_in.shape[1:]
    piece = w_qkv.shape[3]
    z = Sizes(n_dp, images // 2, slots, width, piece)

    x = block_in.reshape(2, z.images, slots, width)
    pg = pred_grad.reshape(2, z.images, slots, width)
    wa = jnp.concatenate([jnp.swapaxes(w_qkv[0], 1, 2).reshape(3 * piece, width), w_out[0]], axis=0)
    res, gin, g_down, g_up, g_attn, small = fused(
        z, x, pg, wa, w_up[0], w_down[0], lengths, patch_mask, qv_bias[0], mlp_bias, norms[0]
    )
    g_qkv = jnp.einsum(
        "id,pod->pio", jnp.eye(width, dtype=BF16), g_attn[:3 * piece].reshape(3, piece, width),
        preferred_element_type=F32,
    )
    g_qv = small[10:12, :piece] + small[12:14, piece:2 * piece]
    return (
        res.reshape(1, images, slots, width),
        gin.reshape(1, images, slots, width).astype(F32),
        g_qkv[None],
        g_attn[3 * piece:].astype(F32)[None],
        g_up.astype(F32)[None],
        g_down.astype(F32)[None],
        g_qv[None],
        small[8:9],
        small[0:8][None],
    )


def solution(mesh):
    return jax.shard_map(
        functools.partial(local, mesh.shape["dp"]),
        mesh=mesh,
        in_specs=(
            P("section", "dp", "tensor", None),
            P("dp"),
            P("dp", None),
            P("dp", "tensor", None),
            P("section", None, None, "tensor"),
            P("section", "tensor", None),
            P("section", None, "tensor"),
            P("section", "tensor", None),
            P("section", None, "tensor"),
            P("section", "tensor"),
            P("section", None, None),
        ),
        out_specs=(
            P("section", "dp", "tensor", None),
            P("section", "dp", "tensor", None),
            P("section", None, None, "tensor"),
            P("section", "tensor", None),
            P("section", None, "tensor"),
            P("section", "tensor", None),
            P("section", None, "tensor"),
            P("section", "tensor"),
            P("section", None, None),
        ),
        check_vma=False,
    )
```

time: 302 us -> 248 us (0.82)
  Pallas kernels: 279 us -> 233 us
  local copies, waits for them, and re-layouts: 9.2 us -> 2.49 us
  other arithmetic: 12.8 us -> 9.23 us
    pallas_call x1, Pallas kernels: 279 us -> 233 us  [fused(): pl.pallas_call(functools.partial(body, z, places), out_shape=(rows, rows,...]
where the time goes in v2:
time: 248 us
  Pallas kernels  233 us (94%)
  other arithmetic  9.23 us (4%)
  local copies, waits for them, and re-layouts  2.49 us (1%)
    pallas_call x1, Pallas kernels, fused(): pl.pallas_call(functools.partial(body, z, places), out_shape=(rows, rows,...  233 us

profile of v2, /device:TPU:0, one launch (start us, length us, event | category | flops | bytes accessed | tf_op | source)
XLA Modules:
  0.0 247.8 jit_solution(17221178600645277145)
XLA Ops:
  0.6 2.4 pad_maximum_fusion.wa_ref
  3.0 233.3 %shard_map.178 = (bf16[2,3,64,768]{3,2,1,0:T(8,128)(2,1)}, bf16[2,3,64,768]{3,2,1,0:T(8,128)(2,1)}, bf16[768,768]{1,0:T(8,128)(2,1)}, bf16[768,768]{1,0:T(8,128)...) custom-call(bf16[2,3,64,768]{3,2,1,0:T(8,128)(2,1)} %bitcast.45, bf16[2,3,64,768]{3,2,1,0:T(8,128)(2,1)} %bitcast.46, ...), custom_call_target="tpu_custom_call" | custom-call | tf_op jit(solution)/shard_map/pallas_call | solution.py:962
  236.3 0.0 copy-start.3
  236.3 0.0 copy-start
  236.3 4.3 %bitcast_convert_fusion = (f32[1,768,768]{2,1,0:T(8,128)}, f32[1,768,768]{2,1,0:T(8,128)}) fusion(bf16[768,768]{1,0:T(8,128)(2,1)} %get-tuple-element.19, bf16[768,768]{1,0:T(8,128)(2,1)} %get-tuple-element.18), kind=kLoop, calls=%fused_computation.5 | loop fusion | flops 1179648 | bytes 7077888 | tf_op jit(solution)/shard_map/broadcast_in_dim | solution.py:999
  240.6 0.0 copy-done.3
  240.6 0.6 slice_bitcast_fusion
  241.2 0.6 slice.22
  241.8 0.7 add_bitcast_fusion
  242.4 0.0 copy-done
  242.5 0.1 slice.18
  242.5 2.1 fusion.3
  244.6 0.0 copy-start.1
  244.6 0.0 copy-start.2
  244.6 0.9 bitcast_convert_fusion.3
  245.4 0.4 copy-done.1
  245.8 1.1 bitcast_convert_fusion.2
  247.0 0.0 copy-done.2
  247.0 0.8 copy.21
Async XLA Ops:
  236.3 4.3 %copy-start.3 = (f32[16,768]{1,0:T(8,128)S(1)}, f32[16,768]{1,0:T(8,128)}, u32[]{:S(2)}) copy-start(f32[16,768]{1,0:T(8,128)} %get-tuple-element.20) | copy-start | bytes 147460
  236.3 6.1 %copy-start = (bf16[768,768]{1,0:T(8,128)(2,1)S(1)}, bf16[768,768]{1,0:T(8,128)(2,1)}, u32[]{:S(2)}) copy-start(bf16[768,768]{1,0:T(8,128)(2,1)} %get-tuple-element.17) | copy-start | bytes 3538948
  244.6 1.3 copy-start.1
  244.6 2.4 copy-start.2

commit v3 on v2

--- a/solution.py
+++ b/solution.py
@@ -10,7 +10,8 @@
 HD = 64
 CH = 128
 GC = 64
-AROUND = (2, 1, 1)
+AROUND = (1, 1, 1)
+HELP_E = (3, 2, 2)
 EPS = 1e-06
 MASKED = -1000000000.0
 F32 = jnp.float32
@@ -82,22 +83,22 @@
         d1=p.take(z.around), d2=p.take(z.around),
         e=p.take(z.images), ec=p.take(z.images),
         attn=p.take(z.images), h2=p.take(z.images), br=p.take(z.images), dbl=p.take(z.images),
-        dh2=p.take(), dal=p.take(), dn=p.take(z.images),
+        dh2=p.take(), dal=p.take(z.images), dn=p.take(z.images),
         dlat=p.take(z.images), res=p.take(), gin=p.take(),
         gy=p.take(z.parts), ga=p.take(z.parts), gb=p.take(z.parts),
         sy=p.take(), sc=p.take(), sa=p.take(), sb=p.take(),
     )
-    together = ("wy", "wz", "d1", "gy", "ga", "gb", "attn", "h2", "br", "dbl", "e", "ec", "dlat", "dn")
+    together = ("wy", "wz", "d1", "gy", "ga", "gb", "attn", "h2", "br", "dbl", "e", "ec", "dlat", "dn", "dal")
     many = dict(bias=2, d2=z.around)
     send = {name: d.take(many.get(name, 1)) for name in recv}
     send["d3"] = d.take(z.around)
-    local = {name: n.take() for name in ("w0", "w1", "w2", "x", "pg", "res", "gin", "g0", "g1", "g2")}
+    local = {name: n.take() for name in ("w0", "wo", "w1", "w2", "x", "pg", "res", "gin", "g0", "g1", "g2")}
     return recv, send, frozenset(together), local, p.count, d.count, n.count
 
 
 def body(
     z, places,
-    x_ref, pg_ref, wa_ref, wu_ref, wd_ref, len_ref, mask_ref, qv_ref, mlp_ref, norm_ref,
+    x_ref, pg_ref, wqkv_ref, wout_ref, wu_ref, wd_ref, len_ref, mask_ref, qv_ref, mlp_ref, norm_ref,
     res_ref, gin_ref, gd_ref, gu_ref, ga_ref, small_ref,
     wown, wy, xall, pgr, qv_y, mlp_y, code_c, seen_c, cov_c, key_r,
     e_own, e_oth, h, kv, q, kk, vv, o, p, att, mid, h2, act, gp, brv, dy,
@@ -129,7 +130,8 @@
     PC, PW = z.piece, z.pair
     KEYS = 2 * BL
     WP = D // CH
-    HELP = (2, WP // 2)
+    HELP = (HELP_E, (WP // 2,) * 3)
+    MOST = WP // 2
 
     def far(src, dst, name, to, index=0, receive=None, send=None):
         leave = SEND[send or name] + (0 if name in TOGETHER else index)
@@ -144,12 +146,12 @@
     def here(src, dst, name):
         return pltpu.make_async_copy(src, dst, ls.at[LOCAL[name]])
 
-    w_refs = (wa_ref, wu_ref, wd_ref)
-    own_w = [here(w_refs[m], wown.at[m], ("w0", "w1", "w2")[m]) for m in range(3)]
+    w_refs = (wown.at[0], wu_ref, wd_ref)
+    own_w = [here(w_refs[m], wown.at[m], ("w0", "w1", "w2")[m]) for m in (1, 2)]
+    own_a = (here(wqkv_ref, wown.at[0, 0:3 * z.piece], "w0"), here(wout_ref, wown.at[0, 3 * z.piece:], "wo"))
     own_x = here(x_ref.at[y], xall.at[0, :, 0], "x")
     own_pg = here(pg_ref.at[y], pgr.at[0], "pg")
-    own_x.start()
-    for copy in own_w:
+    for copy in (own_x, *own_a, *own_w):
         copy.start()
     own_pg.start()
 
@@ -190,7 +192,7 @@
         at = rows_of(j, parity if side is None else side)
         return far(wy.at[m, at], wy.at[m, at], "wz", pair_z, m * (WP // 2) + j)
 
-    around = [(m, WP - HELP[0] - 1 - j) for m in range(3) for j in range(AROUND[m] - 1, -1, -1)]
+    around = [(m, WP - HELP[0][m] - 1 - j) for m in range(3) for j in range(AROUND[m] - 1, -1, -1)]
 
     def d_slot(side, n):
         return g.at[side, pl.ds(n * CH, CH)]
@@ -212,24 +214,32 @@
         )
 
     straight = (
-        [[j for j in range(WP - HELP[0]) if (m, j) not in around] for m in range(3)],
-        [list(range(WP - HELP[1])) for m in range(3)],
+        [[j for j in range(WP - HELP[0][m]) if (m, j) not in around] for m in range(3)],
+        [list(range(WP - HELP[1][m])) for m in range(3)],
     )
 
     def start_inputs():
+        c_xc0.start()
         c_x.start()
         c_b0.start()
         c_b1.start()
-        c_xc0.start()
+
+    @pl.when(reg)
+    def _():
+        start_inputs()
+
+    for copy in own_a:
+        copy.wait()
 
     @pl.when(enc)
     def _():
         for n in range(len(around)):
             d_out(n).start()
-        start_inputs()
         for m in range(3):
             for j in straight[0][m]:
                 w_y(m, j).start()
+                if (m, j) == (0, 1):
+                    start_inputs()
 
     @pl.when(reg)
     def _():
@@ -241,7 +251,6 @@
                 d_over(n - 1).wait_recv()
                 d_back(n - 1).start()
             if n == max(len(around) - 1, 0):
-                start_inputs()
                 for m in range(3):
                     for j in straight[1][m]:
                         w_y(m, j).start()
@@ -250,20 +259,21 @@
             d_over(n).wait_send()
             d_back(n).wait_send()
 
-    def forward_w(m, j):
+    def forward_w(m, j, sections=(enc, reg)):
         for s, flag in enumerate((enc, reg)):
-            @pl.when(jnp.logical_and(flag, j < HELP[s]))
-            def _():
-                w_y(m, j).wait_recv()
-                w_z(m, j).start()
+            if any(flag is one for one in sections) and j < HELP[s][m]:
+                @pl.when(flag)
+                def _():
+                    w_y(m, j).wait_recv()
+                    w_z(m, j).start()
 
     def finish_w(m):
         for s, flag in enumerate((enc, reg)):
             @pl.when(flag)
             def _():
-                for j in range(HELP[s], WP - HELP[s]):
+                for j in range(HELP[s][m], WP - HELP[s][m]):
                     w_y(m, j).wait_recv()
-                for j in range(HELP[s]):
+                for j in range(HELP[s][m]):
                     w_z(m, j, 1 - parity).wait_recv()
 
     rank = lax.broadcasted_iota(jnp.int32, (KEYS, KEYS), 0)
@@ -292,6 +302,8 @@
     def lay(block):
         return block.reshape(BL, D)
 
+    forward_w(0, 0)
+    forward_w(0, 1)
     own_x.wait()
     c_x.wait_recv()
     c_xc1.start()
@@ -310,11 +322,10 @@
     c_xc0.wait_recv()
     c_xc1.wait_recv()
     norm_rows(1)
-    for j in range(HELP[1]):
+    for j in range(2, MOST):
         forward_w(0, j)
     c_b0.wait_recv()
     c_b1.wait_recv()
-    own_w[0].wait()
     finish_w(0)
 
     def both_rows(first, many):
@@ -446,31 +457,68 @@
     def other_up(i):
         up(i, 1, wy.at[1], mlp_y)
 
-    for i in range(I + 2):
-        if i < I:
-            attend(i)
-            if i < 2:
-                for j in range(i * HELP[1] // 2, (i + 1) * HELP[1] // 2):
-                    forward_w(1, j)
-            middle(i)
+    def own_back(i):
+        @pl.when(reg)
+        def _():
+            dy[i] = jnp.concatenate([pgr[0, i], pgr[1, i]], axis=0).astype(F32) * cov_c[i, :BL]
+
+        @pl.when(enc)
+        def _():
+            d_hop(i).wait_recv()
+            dy[i] = dlat[1, i].astype(F32) * seen_c[i, :BL]
+
+        dbl[0, i] = (norm_ref[7:8, :] * dy[i]).astype(BF16)
+        dbl_core(i).start()
+
+    def d_hop(i):
+        return far(dlat.at[0, i], dlat.at[1, i], "dlat", to_s, i)
+
+    def dbl_core(i):
+        return far(dbl.at[0, i], dbl.at[1, i], "dbl", to_c, i)
+
+    for j in range(MOST):
+        forward_w(1, j, (reg,))
+    forward_w(2, 0, (reg,))
+
+    for i in range(I):
+        attend(i)
+        if i == 0:
+            forward_w(1, 0, (enc,))
+            forward_w(1, 1, (enc,))
+            forward_w(2, 1, (reg,))
         if i == 1:
-            own_w[1].wait()
-        if 1 <= i <= I:
-            own_up(i - 1)
-            for j in range((i - 1) * HELP[1] // I, i * HELP[1] // I):
-                forward_w(2, j)
-            if i == 1:
-                finish_w(1)
-            other_up(i - 1)
-        if i == I:
-            own_w[2].wait()
-            finish_w(2)
-            for n in range(I - 1):
-                down(n)
-        if i == I + 1:
-            down(I - 1)
-            for n in range(I):
-                finish(n)
+            forward_w(1, 2, (enc,))
+            forward_w(2, 2, (reg,))
+        if i > 0:
+            middle(i - 1)
+    forward_w(2, 0, (enc,))
+    own_w[0].wait()
+    own_up(0)
+    middle(I - 1)
+    forward_w(2, 1, (enc,))
+    for i in range(1, I):
+        own_up(i)
+        if i < MOST - 1:
+            forward_w(2, i + 1, (enc,))
+    finish_w(1)
+    for i in range(I):
+        other_up(i)
+
+    own_pg.wait()
+
+    @pl.when(reg)
+    def _():
+        c_pg.wait_recv()
+        for i in range(I):
+            own_back(i)
+
+    own_w[1].wait()
+    finish_w(2)
+    for i in range(I):
+        down(i)
+        if i > 0:
+            finish(i - 1)
+    finish(I - 1)
     w_o = both_rows(3 * PC, PC)
 
     def deliver(which, number, ref):
@@ -488,37 +536,17 @@
     def add_norm(row, value):
         nacc[row:row + 1, :] += value
 
-    def d_hop(i):
-        return far(dlat.at[0, i], dlat.at[1, i], "dlat", to_s, i)
-
-    def dbl_core(i):
-        return far(dbl.at[0, i], dbl.at[1, i], "dbl", to_c, i)
-
-    own_pg.wait()
-
-    @pl.when(reg)
-    def _():
-        c_pg.wait_recv()
-
-    def start_back(i, carry):
-        @pl.when(reg)
-        def _():
-            dy[i] = jnp.concatenate([pgr[0, i], pgr[1, i]], axis=0).astype(F32) * cov_c[i, :BL]
-
-        @pl.when(enc)
-        def _():
-            d_hop(i).wait_recv()
-            dy[i] = dlat[1, i].astype(F32) * seen_c[i, :BL]
-
+    @pl.when(enc)
+    def _():
+        for i in range(I):
+            own_back(i)
+
+    def branch_sums(i, carry):
         grad = dy[i]
-        d_branch = norm_ref[7:8, :] * grad
-        dbl[0, i] = d_branch.astype(BF16)
-        dbl_core(i).start()
         add_norm(7, column_sum(grad * brv[i]))
-        add_norm(6, column_sum(d_branch))
+        add_norm(6, column_sum(norm_ref[7:8, :] * grad))
         return carry
 
-    lax.fori_loop(0, I, start_back, 0)
     for i in range(I):
         dbl_core(i).wait_recv()
 
@@ -738,6 +766,7 @@
     snd[0] = up_back(1).astype(BF16).reshape(I, BL, D)
     c_dh2 = far(snd.at[0], rcv.at[2], "dh2", to_c)
     c_dh2.start()
+    lax.fori_loop(0, I, branch_sums, 0)
     pump(1)
     down_back(0, 1, wy.at[2])
     pump(1)
@@ -756,6 +785,9 @@
     pump(1)
     back0 = up_back(0).reshape(I, BL, D)
     c_dh2.wait_recv()
+
+    def dal_core(i):
+        return far(dal.at[0, i], dal.at[1, i], "dal", to_c, i)
 
     for i in range(I):
         grad = back0[i] + rcv[2, i].astype(F32)
@@ -768,13 +800,7 @@
         d_att = norm_ref[3:4, :] * d_mid
         add_norm(2, column_sum(d_att))
         dal[0, i] = d_att.astype(BF16)
-    c_dal = far(dal.at[0], dal.at[1], "dal", to_c)
-    c_dal.start()
-    pump(1)
-
-    dol[0] = nt(flat(dal, 0), w_o).astype(BF16).reshape(I, BL, PW)
-    c_dal.wait_recv()
-    dol[1] = nt(flat(dal, 1), w_o).astype(BF16).reshape(I, BL, PW)
+        dal_core(i).start()
     pump(1)
 
     def all_rows(ref):
@@ -787,6 +813,8 @@
         g[1, base + first:base + first + PC, :] = value[PC:].astype(BF16)
 
     def attend_back(i):
+        dal_core(i).wait_recv()
+        dol[:, i] = nt(dal[:, i].reshape(KEYS, D), w_o).astype(BF16).reshape(2, BL, PW)
         for pr in range(z.heads // 2):
             qp, kp, vp, gpair = image(q, i, pr), image(kk, i, pr), image(vv, i, pr), image(dol, i, pr)
             at = slice(pr * 2 * HD, (pr + 1) * 2 * HD)
@@ -891,10 +919,11 @@
     for which, number, ref in ((0, "res", res_ref), (1, "gin", gin_ref)):
         for copy in deliver(which, number, ref):
             copy.wait()
-    for copy in (c_x, c_b0, c_b1, c_xc0, c_xc1, c_dh2, c_dal):
+    for copy in (c_x, c_b0, c_b1, c_xc0, c_xc1, c_dh2):
         copy.wait_send()
     gone(h2.at[0], "h2", to_c)
     gone(dbl.at[0], "dbl", to_c)
+    gone(dal.at[0], "dal", to_c)
     gone(snd.at[1], "dn", to_c)
 
     @pl.when(enc)
@@ -913,10 +942,10 @@
         @pl.when(flag)
         def _():
             gone(g.at[0, 0:sum(len(js) for js in straight[s]) * CH], "wy", to_y)
-            gone(g.at[0, 0:3 * HELP[s] * CH], "wz", pair_z)
-
-
-def fused(z, x, pg, wa, wu, wd, lengths, mask, qv, mlp, norms):
+            gone(g.at[0, 0:sum(HELP[s]) * CH], "wz", pair_z)
+
+
+def fused(z, x, pg, wqkv, wout, wu, wd, lengths, mask, qv, mlp, norms):
     *places, arrivals, departures, copies = plan(z)
     I, R, D, BL, SL = z.images, z.rows, z.width, z.block, z.slots
     PC, PW = z.piece, z.pair
@@ -962,13 +991,64 @@
     return pl.pallas_call(
         functools.partial(body, z, places),
         out_shape=(rows, rows, weight, weight, weight, jax.ShapeDtypeStruct((16, D), F32)),
-        in_specs=[hbm] * 5 + [sm] + [vm] * 4,
+        in_specs=[hbm] * 6 + [sm] + [vm] * 4,
         out_specs=(hbm, hbm, hbm, hbm, hbm, vm),
         scratch_shapes=scratch,
         compiler_params=pltpu.CompilerParams(
             collective_id=0, has_side_effects=True, vmem_limit_bytes=121 * 2**19
         ),
-    )(x, pg, wa, wu, wd, lengths, mask, qv, mlp, norms)
+    )(x, pg, wqkv, wout, wu, wd, lengths, mask, qv, mlp, norms)
+
+
+def widen(
+    piece, n_qkv,
+    res, gin, gd, gu, ga, small,
+    o_res, o_gin, o_down, o_up, o_qkv, o_out, o_qv, o_mlp, o_norms,
+):
+    n = pl.program_id(0)
+    o_res[...] = res[...]
+    o_gin[...] = gin[...].astype(F32)
+    o_down[...] = gd[...].astype(F32)
+    o_up[...] = gu[...].astype(F32)
+
+    @pl.when(n < n_qkv)
+    def _():
+        o_qkv[...] = ga[...].astype(F32)
+
+    @pl.when(n >= n_qkv)
+    def _():
+        o_out[...] = ga[...].astype(F32)
+
+    @pl.when(n == 0)
+    def _():
+        o_qv[...] = small[10:12, :piece] + small[12:14, piece:2 * piece]
+        o_mlp[...] = small[8:9, :]
+        o_norms[...] = small[0:8, :]
+
+
+def outputs(z, res, gin, gd, gu, ga, small):
+    D, PC = z.width, z.piece
+    tile = 192
+    steps = D // tile
+    n_qkv = 3 * PC // tile
+    token_rows = 2 * z.images * z.slots
+    token_tile = token_rows // steps
+    tokens = pl.BlockSpec((token_tile, D), lambda n: (n, 0))
+    rows = pl.BlockSpec((tile, D), lambda n: (n, 0))
+    once = lambda *shape: pl.BlockSpec(shape, lambda n: (0, 0))
+    first = pl.BlockSpec((tile, D), lambda n: (jnp.minimum(n, n_qkv - 1), 0))
+    last = pl.BlockSpec((tile, D), lambda n: (jnp.maximum(n - n_qkv, 0), 0))
+    shape = jax.ShapeDtypeStruct
+    return pl.pallas_call(
+        functools.partial(widen, PC, n_qkv),
+        grid=(steps,),
+        out_shape=(
+            shape((token_rows, D), BF16), shape((token_rows, D), F32), shape((D, D), F32), shape((D, D), F32),
+            shape((3 * PC, D), F32), shape((PC, D), F32), shape((2, PC), F32), shape((1, D), F32), shape((8, D), F32),
+        ),
+        in_specs=[tokens, tokens, rows, rows, rows, once(16, D)],
+        out_specs=(tokens, tokens, rows, rows, first, last, once(2, PC), once(1, D), once(8, D)),
+    )(res.reshape(token_rows, D), gin.reshape(token_rows, D), gd, gu, ga, small)
 
 
 def local(
@@ -981,25 +1061,21 @@
 
     x = block_in.reshape(2, z.images, slots, width)
     pg = pred_grad.reshape(2, z.images, slots, width)
-    wa = jnp.concatenate([jnp.swapaxes(w_qkv[0], 1, 2).reshape(3 * piece, width), w_out[0]], axis=0)
-    res, gin, g_down, g_up, g_attn, small = fused(
-        z, x, pg, wa, w_up[0], w_down[0], lengths, patch_mask, qv_bias[0], mlp_bias, norms[0]
+    wqkv = jnp.swapaxes(w_qkv[0], 1, 2).reshape(3 * piece, width)
+    summed = fused(
+        z, x, pg, wqkv, w_out[0], w_up[0], w_down[0], lengths, patch_mask, qv_bias[0], mlp_bias, norms[0]
     )
-    g_qkv = jnp.einsum(
-        "id,pod->pio", jnp.eye(width, dtype=BF16), g_attn[:3 * piece].reshape(3, piece, width),
-        preferred_element_type=F32,
-    )
-    g_qv = small[10:12, :piece] + small[12:14, piece:2 * piece]
+    res, gin, g_down, g_up, g_qkv, g_out, g_qv, g_mlp, g_norms = outputs(z, *summed)
     return (
         res.reshape(1, images, slots, width),
-        gin.reshape(1, images, slots, width).astype(F32),
-        g_qkv[None],
-        g_attn[3 * piece:].astype(F32)[None],
-        g_up.astype(F32)[None],
-        g_down.astype(F32)[None],
+        gin.reshape(1, images, slots, width),
+        jnp.swapaxes(g_qkv.reshape(3, piece, width), 1, 2)[None],
+        g_out[None],
+        g_up[None],
+        g_down[None],
         g_qv[None],
-        small[8:9],
-        small[0:8][None],
+        g_mlp,
+        g_norms[None],
     )
 
 

time: 248 us -> 223 us (0.90)
  Pallas kernels: 233 us -> 222 us
  other arithmetic: 9.23 us -> 0 us
  local copies, waits for them, and re-layouts: 2.49 us -> 0 us
    pallas_call x1, Pallas kernels: 233 us -> 215 us  [fused(): pl.pallas_call(functools.partial(body, z, places), out_shape=(rows, rows,...]
    pallas_call x0 -> x1, Pallas kernels: none -> 6.57 us  [outputs(): pl.pallas_call(functools.partial(widen, PC, n_qkv), grid=(steps,), out_sh...]
    broadcast_in_dim x3 -> x0, other arithmetic: 5.77 us -> none  [the longest x1 4.27 us: local(): g_down.astype(F32)[None]]
where the time goes in v3:
time: 223 us
  Pallas kernels  222 us (100%)
    pallas_call x1, Pallas kernels, fused(): pl.pallas_call(functools.partial(body, z, places), out_shape=(rows, rows,...  215 us
    pallas_call x1, Pallas kernels, outputs(): pl.pallas_call(functools.partial(widen, PC, n_qkv), grid=(steps,), out_sh...  6.57 us

profile of v3, /device:TPU:0, one launch (start us, length us, event | category | flops | bytes accessed | tf_op | source)
XLA Modules:
  0.0 222.6 jit_solution(7753646041172014791)
XLA Ops:
  0.6 215.2 %shard_map.178 = (bf16[2,3,64,768]{3,2,1,0:T(8,128)(2,1)}, bf16[2,3,64,768]{3,2,1,0:T(8,128)(2,1)}, bf16[768,768]{1,0:T(8,128)(2,1)}, bf16[768,768]{1,0:T(8,128)...) custom-call(bf16[2,3,64,768]{3,2,1,0:T(8,128)(2,1)} %bitcast.29, bf16[2,3,64,768]{3,2,1,0:T(8,128)(2,1)} %bitcast.30, ...), custom_call_target="tpu_custom_call" | custom-call | tf_op jit(solution)/shard_map/pallas_call | solution.py:991
  215.9 6.6 %shard_map.179 = (bf16[384,768]{1,0:T(8,128)(2,1)}, f32[384,768]{1,0:T(8,128)}, f32[768,768]{1,0:T(8,128)}, f32[768,768]{1,0:T(8,128)}, f32[576,768]{1,0:T(8,128...) custom-call(bf16[384,768]{1,0:T(8,128)(2,1)} %bitcast.31, ...), custom_call_target="tpu_custom_call" | custom-call | tf_op jit(solution)/shard_map/pallas_call | solution.py:1042
